TPU v7x, 32 devices: a whole 2x2x4 slice. The times are simulated.
32 devices in a mesh: rep: 2 (over y), req: 4 (over x, core), tp: 4 (over z).
Axes of the slice: x: 2, y: 2, z: 4, core: 2. Of those that a mesh axis runs over, the one named last changes fastest.
Arguments:
- hidden: bfloat16 [64, 8192], P(('rep', 'req'), 'tp'), parts along dimension 0, may hold values from -6 to 6
- value_projection_weight: bfloat16 [8192, 1024], P('tp'), may hold values from -0.0625 to 0.0625
- adapter_down_weight: bfloat16 [4096, 16, 8192], P(('rep', 'req'), None, 'tp'), parts along dimension 0, may hold values from -0.0625 to 0.0625
- adapter_up_weight: bfloat16 [4096, 16, 1024], P(('rep', 'req'), None, 'tp'), parts along dimension 0, may hold values from -1.5 to 1.5
- adapter_store_row: int32 [4096], P('rep'), parts along dimension 0, may hold values from 0 to 2047, as said below
- request_group_adapters: int32 [64], P(('rep', 'req')), parts along dimension 0, may hold values from 0 to 2047, as said below
- row_list_entry: int32 [64, 1], P(('rep', 'req')), parts along dimension 0, may hold values from 0 to 7
- cache_length: int32 [64], P(('rep', 'req')), parts along dimension 0, may hold values from 2 to 512, as said below
- query: bfloat16 [64, 8192], P(('rep', 'req')), parts along dimension 0, may hold values from -6 to 6
- cached_key_rows: bfloat16 [64, 512, 1024], P(('rep', 'req'), 'tp'), parts along dimension 0, may hold values from -6 to 6
- cached_value_rows: bfloat16 [64, 512, 1024], P(('rep', 'req'), 'tp'), parts along dimension 0, may hold values from -6 to 6
- new_token_keys: bfloat16 [64, 1024], P(('rep', 'req')), parts along dimension 0, may hold values from -6 to 6
Outputs:
- value_new: bfloat16 [64, 1024], P(('rep', 'req')), parts along dimension 0
- attention_out: bfloat16 [64, 8192], P(('rep', 'req'), 'tp'), parts along dimension 0
There are 2 independent parts, one for each index of `rep`. A program takes and returns all parts, laid end to end along the dimension named above; an argument that names none is the same for every part. Nothing has to cross between parts.
Inputs may be any that keep to these rules, and one draw needn't show every extreme that they name: A permutation: adapter a lives at store row adapter_store_row[a] of adapter_down_weight and adapter_up_weight, that is in the store of request group adapter_store_row[a] // 512. `request_group_adapters`: each group's 8 entries are distinct adapter ids; at most 2 of one group's entries live in one request group's store, and in every group some store holds exactly 2 of them. `row_list_entry`: an index into the row's own group's list. `cache_length`: some row has a full cache.
All inputs are finite; a program needn't handle non-finite values.
Results may differ from a plain program's by a relative error of at most 0.0041.
Values may be sent and summed in bfloat16 or wider, within the bound.
A program may use at most 128 MiB of HBM per device.

v0:
```python
import jax
import jax.numpy as jnp
from jax import lax
from jax.sharding import PartitionSpec as P

HD = 128
ADAPTER_RANK = 16
CAP = 2


masked_score = -1e30


def joined(value, axis, combine):
    everything = jax.tree.map(lambda part: lax.all_gather(part, axis), value)
    first = jax.tree.map(lambda part: part[0], everything)

    def step(k, so_far):
        return combine(so_far, jax.tree.map(lambda part: part[k], everything))

    return lax.fori_loop(1, lax.axis_size(axis), step, first)


def locate(wanted_ids, adapter_store_row):
    catalog = jnp.arange(adapter_store_row.shape[0], dtype=jnp.int32)
    matches = wanted_ids[:, None] == catalog[None, :]
    return jnp.sum(jnp.where(matches, adapter_store_row[None, :], 0), axis=1)


def per_device(
    hidden,
    value_projection_weight,
    adapter_down_weight,
    adapter_up_weight,
    adapter_store_row,
    request_group_adapters,
    row_list_entry,
    cache_length,
    query,
    cached_key_rows,
    cached_value_rows,
    new_token_keys,
):
    req_count = lax.axis_size("req")
    req_index = lax.axis_index("req")
    tp_index = lax.axis_index("tp")
    group_rows = hidden.shape[0]
    list_len = request_group_adapters.shape[0]
    store_row_index = adapter_down_weight.shape[0]
    kv_width = value_projection_weight.shape[1]
    value_columns = adapter_up_weight.shape[2]
    highest = lax.Precision.HIGHEST
    selected_adapters = row_list_entry == jnp.arange(list_len, dtype=jnp.int32)[None, :]
    base_part = jnp.dot(hidden, value_projection_weight, preferred_element_type=jnp.float32)
    wanted = lax.all_gather(request_group_adapters, "req", axis=0, tiled=True)
    positions = locate(wanted, adapter_store_row).reshape(req_count, list_len)
    owners = positions // store_row_index
    slot_index = positions % store_row_index
    earlier = jnp.arange(list_len)[:, None] > jnp.arange(list_len)[None, :]
    order_index = jnp.sum((owners[:, :, None] == owners[:, None, :]) & earlier[None], axis=2)
    sent_match = (owners == req_index)[:, :, None] & (
        order_index[:, :, None] == jnp.arange(CAP)[None, None, :]
    )
    outgoing_slot = jnp.sum(jnp.where(sent_match, slot_index[:, :, None], 0), axis=1)
    filled_positions = jnp.any(sent_match, axis=1)
    down_outgoing = jnp.where(
        filled_positions[:, :, None, None], adapter_down_weight[outgoing_slot], 0
    )
    up_outgoing = jnp.where(filled_positions[:, :, None, None], adapter_up_weight[outgoing_slot], 0)
    down_recv, up_recv = (
        lax.all_to_all(down_outgoing, "req", split_axis=0, concat_axis=0, tiled=True),
        lax.all_to_all(up_outgoing, "req", split_axis=0, concat_axis=0, tiled=True),
    )
    where_from = jnp.take(owners, req_index, axis=0) * CAP + jnp.take(
        order_index, req_index, axis=0
    )
    down_list = down_recv.reshape(req_count * CAP, ADAPTER_RANK, hidden.shape[1])[where_from]
    up_list = up_recv.reshape(req_count * CAP, ADAPTER_RANK, value_columns)[where_from]
    low_each = jnp.einsum("rd,skd->rsk", hidden, down_list, preferred_element_type=jnp.float32)
    low_part = jnp.sum(jnp.where(selected_adapters[:, :, None], low_each, 0.0), axis=1)
    value_sum, low_rank = lax.psum((base_part, low_part), "tp")
    base_columns = lax.dynamic_slice_in_dim(value_sum, tp_index * value_columns, value_columns, 1)
    up_per_row = jnp.einsum("rk,skc->rsc", low_rank, up_list.astype(jnp.float32), precision=highest)
    adapter_columns = jnp.sum(jnp.where(selected_adapters[:, :, None], up_per_row, 0.0), axis=1)
    local_value_part = (base_columns + adapter_columns).astype(jnp.bfloat16)
    value_new = lax.all_gather(local_value_part, "tp", axis=1, tiled=True)
    heads_total = query.shape[1] // HD
    kv_heads = kv_width // HD
    per_group = heads_total // kv_heads
    heads_here = heads_total // lax.axis_size("tp")
    block_len = cached_key_rows.shape[1]
    scale_factor = HD ** (-0.5)
    queries = query.reshape(group_rows, kv_heads, per_group, HD)
    keys = cached_key_rows.reshape(group_rows, block_len, kv_heads, HD)
    values = cached_value_rows.reshape(group_rows, block_len, kv_heads, HD)
    scores = (
        jnp.einsum("rkgd,rlkd->rkgl", queries, keys, preferred_element_type=jnp.float32)
        * scale_factor
    )
    positions_here = tp_index * block_len + jnp.arange(block_len, dtype=jnp.int32)
    valid = positions_here[None, None, None, :] < cache_length[:, None, None, None]
    scores = jnp.where(valid, scores, masked_score)
    block_max = jnp.max(scores, axis=3)
    probs = jnp.where(valid, jnp.exp(scores - block_max[..., None]), 0.0).astype(jnp.bfloat16)
    block_den = jnp.sum(probs.astype(jnp.float32), axis=3)
    block_acc = jnp.einsum("rkgl,rlkd->rkgd", probs, values, preferred_element_type=jnp.float32)
    fresh_keys = new_token_keys.reshape(group_rows, kv_heads, HD)
    fresh_score = (
        jnp.einsum("rkgd,rkd->rkg", queries, fresh_keys, preferred_element_type=jnp.float32)
        * scale_factor
    )
    fresh_value = jnp.broadcast_to(
        value_new.reshape(group_rows, kv_heads, 1, HD).astype(jnp.float32),
        (group_rows, kv_heads, per_group, HD),
    )

    def combine(first, second):
        peak_both = jnp.maximum(first[0], second[0])
        scale_first = jnp.exp(first[0] - peak_both)
        scale_second = jnp.exp(second[0] - peak_both)
        return (
            peak_both,
            first[1] * scale_first + second[1] * scale_second,
            first[2] * scale_first[..., None] + second[2] * scale_second[..., None],
        )

    merged_max, merged_den, merged_acc = joined((block_max, block_den, block_acc), "tp", combine)
    peak = jnp.maximum(merged_max, fresh_score)
    weight_old = jnp.exp(merged_max - peak)
    weight_new = jnp.exp(fresh_score - peak)
    total_den = merged_den * weight_old + weight_new
    total_acc = merged_acc * weight_old[..., None] + weight_new[..., None] * fresh_value
    attended = (total_acc / total_den[..., None]).reshape(group_rows, heads_total * HD)
    attention_out = lax.dynamic_slice_in_dim(
        attended, tp_index * heads_here * HD, heads_here * HD, 1
    ).astype(jnp.bfloat16)
    return (value_new, attention_out)


def solution(mesh):
    return jax.shard_map(
        per_device,
        mesh=mesh,
        in_specs=(
            P(("rep", "req"), "tp"),
            P("tp", None),
            P(("rep", "req"), None, "tp"),
            P(("rep", "req"), None, "tp"),
            P("rep"),
            P(("rep", "req")),
            P(("rep", "req"), None),
            P(("rep", "req")),
            P(("rep", "req"), None),
            P(("rep", "req"), "tp", None),
            P(("rep", "req"), "tp", None),
            P(("rep", "req"), None),
        ),
        out_specs=(P(("rep", "req"), None), P(("rep", "req"), "tp")),
        check_vma=False,
    )
```

profile of v0, /device:TPU:0, one launch (start us, length us, event | category | flops | bytes accessed | tf_op | source)
XLA Modules:
  0.0 121.0 jit_solution(17376213010681431208)
XLA Ops:
  7.3 0.9 broadcast_compare_fusion
  8.8 2.2 %fusion.37 = (f32[8,8,8]{2,1,0:T(8,128)S(1)}, f32[8,8,8,128]{3,2,1,0:T(8,128)S(1)}) fusion(bf16[8,8,8,128]{3,0,2,1:T(8,128)(2,1)} %bitcast.105, pred[8,128]{1,0:T(8,128)(4,1)S(1)} %broadcast_compare_fusion, bf16[8,128,1024]{2,1,0:T(8,128)(2,1)S(1)} %copy-done), kind=kOutput, calls=%fused_computation.78 | convolution fusion | flops 16973312 | bytes 2493440 | tf_op jit(solution)/shard_map/rkgd,rlkd->rkgl/dot_general | solution.py:97
  11.0 1.4 %fusion.3 = f32[8,8,8,128]{3,2,1,0:T(8,128)} fusion(f32[8,8,8,128]{3,2,1,0:T(8,128)S(1)} %get-tuple-element.221, f32[8,8,8]{2,1,0:T(8,128)S(1)} %get-tuple-element.220, pred[8,128]{1,0:T(8,128)(4,1)S(1)} %broadcast_compare_fusion, bf16[8,128,1024]{2,1,0:T(8,128)(2,1)S(1)} %copy-done.1), kind=kOutput, calls=%fused_computation.12 | convolution fusion | flops 16973824 | bytes 2624512 | tf_op jit(solution)/shard_map/rkgl,rlkd->rkgd/dot_general | solution.py:106
  14.0 6.3 %all-reduce = s32[32]{0:T(128)S(1)} all-reduce(s32[32]{0:T(128)S(1)} %dynamic-update-slice.1), channel_id=1, replica_groups=mesh['rep'=2,'req'=4,'tp'=4] {'req'}, use_global_device_ids=true, to_apply=%add | all-reduce | flops 32 | bytes 256
  21.5 2.9 %gather_fusion.2 = bf16[8,16,256]{2,1,0:T(8,128)(2,1)S(1)} fusion(bf16[512,16,256]{2,1,0:T(8,128)(2,1)} %param.19, s32[1024]{0:T(1024)S(1)} %pad_clamp_fusion.1), kind=kCustom, calls=%fused_computation.2 | custom fusion | bytes 131104 | tf_op jit(solution)/shard_map/gather | solution.py:69
  25.1 3.3 %all-to-all-start.1 = ((bf16[4,2,16,256]{3,2,1,0:T(8,128)(2,1)}), bf16[4,2,16,256]{3,2,1,0:T(8,128)(2,1)S(1)}, u32[]{:S(2)}, u32[]{:S(2)}) async-start(bf16[4,2,16,256]{3,2,1,0:T(8,128)(2,1)} %broadcast_select_fusion.1), calls=%async_computation.1 | async-start | bytes 131072 | tf_op jit(solution)/shard_map/all_to_all | solution.py:72
  28.4 1.6 %gather_fusion = bf16[8,16,2048]{2,1,0:T(8,128)(2,1)S(1)} fusion(bf16[512,16,2048]{2,1,0:T(8,128)(2,1)} %param.18, s32[1024]{0:T(1024)S(1)} %pad_clamp_fusion.1), kind=kCustom, calls=%fused_computation | custom fusion | bytes 1048608 | tf_op jit(solution)/shard_map/gather | solution.py:67
  30.0 0.9 broadcast_select_fusion
  31.2 0.8 fusion.18
  32.1 14.5 %all-gather.1 = f32[32,8,8]{2,1,0:T(8,128)S(1)} all-gather(f32[8,8,8]{2,1,0:T(8,128)S(1)} %convert_reduce_fusion), channel_id=3, replica_groups=mesh['rep'=2,'req'=4,'tp'=4] {'tp'}, dimensions={0}, use_global_device_ids=true | all-gather | bytes 10240 | tf_op jit(solution)/shard_map/all_gather | solution.py:15
  46.6 13.4 %all-gather = f32[32,8,8]{2,1,0:T(8,128)S(1)} all-gather(f32[8,8,8]{2,1,0:T(8,128)S(1)} %get-tuple-element.220), channel_id=2, replica_groups=mesh['rep'=2,'req'=4,'tp'=4] {'tp'}, dimensions={0}, use_global_device_ids=true | all-gather | bytes 10240 | tf_op jit(solution)/shard_map/all_gather | solution.py:15
  60.0 3.5 %all-to-all-start = ((bf16[4,2,16,2048]{3,2,1,0:T(8,128)(2,1)}), bf16[4,2,16,2048]{3,2,1,0:T(8,128)(2,1)S(1)}, u32[]{:S(2)}, u32[]{:S(2)}) async-start(bf16[4,2,16,2048]{3,2,1,0:T(8,128)(2,1)} %broadcast_select_fusion), calls=%async_computation | async-start | bytes 1048576 | tf_op jit(solution)/shard_map/all_to_all | solution.py:71
  63.5 2.8 %fusion.38 = f32[8,1024]{1,0:T(8,128)S(1)} fusion(bf16[8,2048]{1,0:T(8,128)(2,1)S(1)} %copy-done.2, bf16[2048,1024]{1,0:T(8,128)(2,1)} %param.17), kind=kOutput, calls=%fused_computation.79 | convolution fusion | flops 33554432 | bytes 4259840 | tf_op jit(solution)/shard_map/dot_general | solution.py:54
  66.4 1.2 gather_fusion.3
  67.6 4.8 %all-to-all-done = bf16[4,2,16,2048]{3,2,1,0:T(8,128)(2,1)S(1)} async-done(((bf16[4,2,16,2048]{3,2,1,0:T(8,128)(2,1)}), bf16[4,2,16,2048]{3,2,1,0:T(8,128)(2,1)S(1)}, u32[]{:S(2)}, u32[]{:S(2)}) %all-to-all-start) | async-done | bytes 524320 | tf_op jit(solution)/shard_map/all_to_all | solution.py:71
  72.9 0.7 fusion.17
  73.6 19.8 %all-reduce.1 = (f32[8,16]{1,0:T(8,128)S(1)}, f32[8,1024]{1,0:T(8,128)S(1)}) all-reduce(f32[8,16]{1,0:T(8,128)S(1)} %fusion.17, f32[8,1024]{1,0:T(8,128)S(1)} %fusion.38), channel_id=1, replica_groups=mesh['rep'=2,'req'=4,'tp'=4] {'tp'}, use_global_device_ids=true, to_apply=%region_6.8 | all-reduce | flops 8320 | bytes 66560 | tf_op jit(solution)/shard_map/psum | solution.py:81
  93.5 1.0 fusion.15
  94.5 13.1 %all_gather.25 = bf16[8,1024]{1,0:T(8,128)(2,1)S(1)} all-gather(bf16[8,256]{1,0:T(8,128)(2,1)S(1)} %add_convert_fusion), channel_id=1, replica_groups=mesh['rep'=2,'req'=4,'tp'=4] {'tp'}, dimensions={1}, use_global_device_ids=true | all-gather | bytes 20480 | tf_op jit(solution)/shard_map/all_gather | solution.py:86
  107.7 1.0 slice.32
  108.7 3.8 %while.20 = (s32[]{:T(128)}, f32[8,8,8]{2,1,0:T(8,128)S(1)}, f32[8,8,8]{2,1,0:T(8,128)S(1)}, f32[8,8,8,128]{3,2,1,0:T(8,128)S(1)}, f32[4,8,8,8]{3,2,1,0:T(8,128)...) while((s32[]{:T(128)}, f32[8,8,8]{2,1,0:T(8,128)S(1)}, ...), condition=%wide.region_11.13_spmd, body=%wide.region_10.12_spmd.sunk | while | flops 199685 | bytes 807063 | solution.py:21
  108.7 1.2 %fusion.48 = f32[8,8,8,128]{3,2,1,0:T(8,128)S(1)} fusion(f32[4,8,8,8,128]{4,3,2,1,0:T(8,128)} %get-tuple-element.299, s32[]{:T(128)S(6)} %select_n.156, f32[8,8,8,128]{3,2,1,0:T(8,128)S(1)} %get-tuple-element.286, f32[8,8,8]{2,1,0:T(8,128)S(1)} %get-tuple-element.271, f32[8,8,8]{2,1,0:T(8,128)S(1)} %get-tuple-element.272), kind=kLoop, calls=%fused_computation.5.clone.1 | loop fusion | flops 196608 | bytes 790532 | tf_op jit(solution)/shard_map/while/body/eval_jaxpr/add | solution.py:124
  110.0 1.2 %fusion.48 = f32[8,8,8,128]{3,2,1,0:T(8,128)S(1)} fusion(f32[4,8,8,8,128]{4,3,2,1,0:T(8,128)} %get-tuple-element.299, s32[]{:T(128)S(6)} %select_n.156, f32[8,8,8,128]{3,2,1,0:T(8,128)S(1)} %get-tuple-element.286, f32[8,8,8]{2,1,0:T(8,128)S(1)} %get-tuple-element.271, f32[8,8,8]{2,1,0:T(8,128)S(1)} %get-tuple-element.272), kind=kLoop, calls=%fused_computation.5.clone.1 | loop fusion | flops 196608 | bytes 790532 | tf_op jit(solution)/shard_map/while/body/eval_jaxpr/add | solution.py:124
  111.3 1.2 %fusion.48 = f32[8,8,8,128]{3,2,1,0:T(8,128)S(1)} fusion(f32[4,8,8,8,128]{4,3,2,1,0:T(8,128)} %get-tuple-element.299, s32[]{:T(128)S(6)} %select_n.156, f32[8,8,8,128]{3,2,1,0:T(8,128)S(1)} %get-tuple-element.286, f32[8,8,8]{2,1,0:T(8,128)S(1)} %get-tuple-element.271, f32[8,8,8]{2,1,0:T(8,128)S(1)} %get-tuple-element.272), kind=kLoop, calls=%fused_computation.5.clone.1 | loop fusion | flops 196608 | bytes 790532 | tf_op jit(solution)/shard_map/while/body/eval_jaxpr/add | solution.py:124
  (60 shorter events, 6.1 us)
Async XLA Ops:
  7.2 1.6 %copy-start = (bf16[8,128,1024]{2,1,0:T(8,128)(2,1)S(1)}, bf16[8,128,1024]{2,1,0:T(8,128)(2,1)}, u32[]{:S(2)}) copy-start(bf16[8,128,1024]{2,1,0:T(8,128)(2,1)} %param.25) | copy-start | bytes 6291460
  7.2 100.5 %all-gather.5.cloned.1.call-start = ((), (), s32[]{:S(2)}) async-start(), calls=%async_computation.2 | async-start | bytes 1310720 | tf_op jit(solution)/shard_map/all_gather | solution.py:15
  7.2 3.7 %copy-start.1 = (bf16[8,128,1024]{2,1,0:T(8,128)(2,1)S(1)}, bf16[8,128,1024]{2,1,0:T(8,128)(2,1)}, u32[]{:S(2)}) copy-start(bf16[8,128,1024]{2,1,0:T(8,128)(2,1)} %param.26) | copy-start | bytes 6291460
  10.9 1.5 %copy-start.9 = (u32[32]{0:T(128)S(1)}, u32[32]{0:T(128)}, u32[]{:S(2)}) copy-start(u32[32]{0:T(128)} %constant.139) | copy-start | bytes 388
  10.9 2.8 %copy-start.7 = (s32[8]{0:T(128)S(1)}, s32[8]{0:T(128)}, u32[]{:S(2)}) copy-start(s32[8]{0:T(128)} %param.21) | copy-start | bytes 100
  10.9 9.4 %copy-start.5 = (s32[2048]{0:T(1024)S(1)}, s32[2048]{0:T(1024)}, u32[]{:S(2)}) copy-start(s32[2048]{0:T(1024)} %param.20) | copy-start | bytes 24580
  11.0 20.0 %copy-start.8 = (s32[8,1]{0,1:T(1,128)S(1)}, s32[8,1]{0,1:T(1,128)}, u32[]{:S(2)}) copy-start(s32[8,1]{0,1:T(1,128)} %param.22) | copy-start | bytes 100
  12.4 18.8 %copy-start.3 = (bf16[8,8192]{1,0:T(8,128)(2,1)S(1)}, bf16[8,8192]{1,0:T(8,128)(2,1)}, u32[]{:S(2)}) copy-start(bf16[8,8192]{1,0:T(8,128)(2,1)} %param.24) | copy-start | bytes 393220
  12.4 18.8 %copy-start.6 = (bf16[8,1024]{1,0:T(8,128)(2,1)S(1)}, bf16[8,1024]{1,0:T(8,128)(2,1)}, u32[]{:S(2)}) copy-start(bf16[8,1024]{1,0:T(8,128)(2,1)} %param.27) | copy-start | bytes 49156
  25.1 35.0 %all-to-all-start.1 = ((bf16[4,2,16,256]{3,2,1,0:T(8,128)(2,1)}), bf16[4,2,16,256]{3,2,1,0:T(8,128)(2,1)S(1)}, u32[]{:S(2)}, u32[]{:S(2)}) async-start(bf16[4,2,16,256]{3,2,1,0:T(8,128)(2,1)} %broadcast_select_fusion.1), calls=%async_computation.1 | async-start | bytes 131072 | tf_op jit(solution)/shard_map/all_to_all | solution.py:72
  28.4 35.2 %copy-start.2 = (bf16[8,2048]{1,0:T(8,128)(2,1)S(1)}, bf16[8,2048]{1,0:T(8,128)(2,1)}, u32[]{:S(2)}) copy-start(bf16[8,2048]{1,0:T(8,128)(2,1)} %param.16) | copy-start | bytes 98308
  60.0 12.3 %all-to-all-start = ((bf16[4,2,16,2048]{3,2,1,0:T(8,128)(2,1)}), bf16[4,2,16,2048]{3,2,1,0:T(8,128)(2,1)S(1)}, u32[]{:S(2)}, u32[]{:S(2)}) async-start(bf16[4,2,16,2048]{3,2,1,0:T(8,128)(2,1)} %broadcast_select_fusion), calls=%async_computation | async-start | bytes 1048576 | tf_op jit(solution)/shard_map/all_to_all | solution.py:71
  108.7 3.9 %copy-start.4 = (f32[8,8,1,8]{3,2,1,0:T(1,128)S(1)}, f32[8,8,1,8]{3,2,1,0:T(1,128)}, u32[]{:S(2)}) copy-start(f32[8,8,1,8]{3,2,1,0:T(1,128)} %fusion.18) | copy-start | bytes 6148
Sparse Core Ops, SparseCore 0:
  12.6 32.2 all-gather.4
where the time goes:
time: 122 us; the launch traced here: 121 us
  blocking collectives  67.3 us (55%)
  between operations  15 us (12%)
  local copies, waits for them, and re-layouts  10.5 us (9%)
  matrix products  8.97 us (7%)
  other arithmetic  7.62 us (6%)
  starting transfers between devices  6.8 us (6%)
  waiting for transfers between devices  4.81 us (4%)
    all_gather x2, blocking collectives, joined(): everything = jax.tree.map(lambda part: lax.all_gather(part, axis), value)  27.9 us
    psum x1, blocking collectives, per_device(): value_sum, low_rank = lax.psum((base_part, low_part), 'tp')  19.8 us
    all_gather x1, blocking collectives, per_device(): value_new = lax.all_gather(local_value_part, 'tp', axis=1, tiled=True)  13.1 us
    unnamed x1, blocking collectives  6.35 us
    all_to_all x1, waiting for transfers between devices, per_device(): lax.all_to_all(down_outgoing, 'req', split_axis=0, concat_axis=0, tiled=T...  4.77 us
    add x3, other arithmetic, combine(): first[2] * scale_first[..., None] + second[2] * scale_second[..., None]  3.64 us
    all_to_all x1, starting transfers between devices, per_device(): lax.all_to_all(down_outgoing, 'req', split_axis=0, concat_axis=0, tiled=T...  3.48 us
    all_to_all x1, starting transfers between devices, per_device(): lax.all_to_all(up_outgoing, 'req', split_axis=0, concat_axis=0, tiled=True)  3.28 us
  transfers between devices with their start and end apart: 3, of which 1 were waited for; matrix products, arithmetic and copies ran while one was open for 13% of the time, Pallas kernels for 0%

commit v1 on v0

v1 whole, which is shorter than its diff:
```python
import functools

import jax
import jax.numpy as jnp
from jax import lax
from jax.experimental import pallas as pl
from jax.experimental.pallas import tpu as pltpu
from jax.sharding import PartitionSpec as P

HD = 128
ADAPTER_RANK = 16
CAP = 2
MASKED = -1e30
F32 = jnp.float32
BF16 = jnp.bfloat16
MESH = pl.DeviceIdType.MESH
VMEM = pl.BlockSpec(memory_space=pltpu.VMEM)
SMEM = pl.BlockSpec(memory_space=pltpu.SMEM)
ANY = pl.BlockSpec(memory_space=pl.ANY)


def dot_nt(a, b):
    return lax.dot_general(a, b, (((1,), (1,)), ((), ())), preferred_element_type=F32)


def request_kernel(groups, ids_ref, hidden_ref, ids_out, hidden_out, send_sems, recv_sems):
    me = lax.axis_index("req")
    half = hidden_ref.shape[1] // 2
    barrier = pltpu.get_barrier_semaphore()

    def greet(d, _):
        peer = lax.rem(me + d, groups)
        pl.semaphore_signal(barrier, inc=1, device_id={"req": peer}, device_id_type=MESH)
        return 0

    lax.fori_loop(1, groups, greet, 0)
    wide = hidden_ref[...].astype(F32)
    hidden_out[me] = jnp.concatenate([wide[:, :half], wide[:, half:]], axis=0).astype(BF16)
    ids_out[me] = ids_ref[...]
    pl.semaphore_wait(barrier, groups - 1)

    def copies(d):
        peer = lax.rem(me + d, groups)
        return [
            pltpu.make_async_remote_copy(
                src_ref=ref.at[me],
                dst_ref=ref.at[me],
                send_sem=send_sems.at[n, d],
                recv_sem=recv_sems.at[n, d],
                device_id={"req": peer},
                device_id_type=MESH,
            )
            for n, ref in enumerate((ids_out, hidden_out))
        ]

    def start(d, _):
        for copy in copies(d):
            copy.start()
        return 0

    def finish(d, _):
        for copy in copies(d):
            copy.wait()
        return 0

    lax.fori_loop(1, groups, start, 0)
    lax.fori_loop(1, groups, finish, 0)


def local_kernel(
    groups,
    parts,
    ids,
    table,
    lengths,
    hidden_all,
    hidden,
    query,
    new_keys,
    weight,
    down,
    up,
    keys,
    values,
    low_out,
    up_out,
    base_out,
    acc_out,
    stats_out,
    fresh_out,
    key_buf,
    value_buf,
    weight_buf,
    down_buf,
    slots,
    key_sems,
    value_sems,
    weight_sems,
    down_sems,
    up_sems,
):
    me = lax.axis_index("req")
    tp = lax.axis_index("tp")
    rows, depth = hidden.shape
    kv_width = new_keys.shape[1]
    kv_heads = kv_width // HD
    heads = query.shape[1] // HD
    per = heads // kv_heads
    here = heads // parts
    block = keys.shape[1]
    store = down.shape[0]
    entries = ids.shape[1]
    scale = HD ** (-0.5)

    chunks = key_sems.shape[0]
    wide = kv_width // chunks
    pieces = weight_sems.shape[0]
    tall = depth // pieces

    def key_copy(c):
        part = pl.ds(c * wide, wide)
        return pltpu.make_async_copy(keys.at[:, :, part], key_buf.at[:, :, part], key_sems.at[c])

    def value_copy(c):
        part = pl.ds(c * wide, wide)
        return pltpu.make_async_copy(
            values.at[:, :, part], value_buf.at[:, :, part], value_sems.at[c]
        )

    def weight_copy(c):
        part = pl.ds(c * tall, tall)
        return pltpu.make_async_copy(weight.at[part, :], weight_buf.at[part, :], weight_sems.at[c])

    def down_copy(place, slot):
        part = pl.ds(slot * ADAPTER_RANK, ADAPTER_RANK)
        return pltpu.make_async_copy(down.at[place], down_buf.at[part, :], down_sems.at[slot])

    def up_copy(place, slot):
        part = pl.ds(slot * ADAPTER_RANK, ADAPTER_RANK)
        return pltpu.make_async_copy(up.at[place], up_out.at[part, :], up_sems.at[slot])

    for c in range(chunks):
        key_copy(c).start()
        value_copy(c).start()
    for c in range(pieces):
        weight_copy(c).start()

    up_out[...] = jnp.zeros_like(up_out)
    counts = []
    for g in range(groups):
        count = jnp.int32(0)
        for e in range(entries):
            at = table[ids[g, e, 1]]
            mine = (at // store == me) & (count < CAP)
            slot = g * CAP + count
            slots[g * entries + e] = jnp.where(mine, slot, -1)

            @pl.when(mine)
            def _():
                down_copy(lax.rem(at, store), slot).start()
                up_copy(lax.rem(at, store), slot).start()

            count = count + mine.astype(jnp.int32)
        counts.append(count)

    lane = lax.broadcasted_iota(jnp.int32, (rows, 128), 1)
    sub = lax.broadcasted_iota(jnp.int32, (rows, block), 0)
    length = jnp.zeros((rows, block), jnp.int32)
    for r in range(rows):
        length = jnp.where(sub == r, lengths[r], length)
    position = tp * block + lax.broadcasted_iota(jnp.int32, (rows, block), 1)
    valid_one = (position < length).astype(jnp.int32)
    valid = jnp.concatenate([valid_one] * per, axis=0) > 0

    def own_row(width):
        shape = (per * rows, rows * width)
        row = lax.rem(lax.broadcasted_iota(jnp.int32, shape, 0), rows)
        col = lax.broadcasted_iota(jnp.int32, shape, 1) // width
        return jnp.where(row == col, 1.0, 0.0).astype(BF16)

    own_key = own_row(HD)
    lined = block % 128 == 0
    own_prob = own_key if block == HD else own_row(block) if lined else None
    row_of = lax.rem(lax.broadcasted_iota(jnp.int32, (per * rows, block), 0), rows)

    peaks = [jnp.zeros((rows, 128), F32) for _ in range(parts)]
    sums = [jnp.zeros((rows, 128), F32) for _ in range(parts)]
    for k in range(kv_heads):
        if (k * HD) % wide == 0:
            key_copy(k * HD // wide).wait()
            value_copy(k * HD // wide).wait()
        cols = slice(k * HD, (k + 1) * HD)
        q = jnp.concatenate(
            [
                query[:, (k * per + g) * HD : (k * per + g + 1) * HD].astype(F32)
                for g in range(per)
            ],
            axis=0,
        ).astype(BF16)
        q_wide = jnp.concatenate([q] * rows, axis=1) * own_key
        k_wide = jnp.concatenate([key_buf[r, :, cols] for r in range(rows)], axis=1)
        score = dot_nt(q_wide, k_wide) * scale
        score = jnp.where(valid, score, MASKED)
        peak = jnp.max(score, axis=1, keepdims=True)
        prob = jnp.where(valid, jnp.exp(score - peak), 0.0).astype(BF16)
        prob_f32 = prob.astype(F32)
        total = jnp.sum(prob_f32, axis=1, keepdims=True)
        if lined:
            p_wide = jnp.concatenate([prob] * rows, axis=1) * own_prob
            v_tall = value_buf[:, :, cols].reshape(rows * block, HD)
            acc = jnp.dot(p_wide, v_tall, preferred_element_type=F32)
        else:
            acc = jnp.zeros((per * rows, HD), F32)
            for r in range(rows):
                p_row = jnp.where(row_of == r, prob_f32, 0.0).astype(BF16)
                acc = acc + jnp.dot(p_row, value_buf[r, :, cols], preferred_element_type=F32)
        step = min(per, here)
        for c in range(per // step):
            first = k * per + c * step
            acc_out[first // here, (first % here) * rows : (first % here + step) * rows, :] = acc[
                c * step * rows : (c + 1) * step * rows
            ].astype(BF16)
        for g in range(per):
            head = k * per + g
            part = slice(g * rows, (g + 1) * rows)
            hit = lane == head % here
            peaks[head // here] = jnp.where(hit, peak[part], peaks[head // here])
            sums[head // here] = jnp.where(hit, total[part], sums[head // here])
    for p in range(parts):
        stats_out[p, :rows] = peaks[p]
        stats_out[p, rows:] = sums[p]

    fresh = jnp.zeros((rows, 128), F32)
    for j in range(here):
        head = tp * here + j
        q_at = pl.multiple_of(head * HD, HD)
        k_at = pl.multiple_of(head // per * HD, HD)
        both = query[:, pl.ds(q_at, HD)].astype(F32) * new_keys[:, pl.ds(k_at, HD)].astype(F32)
        fresh = jnp.where(lane == j, jnp.sum(both, axis=1, keepdims=True) * scale, fresh)
    fresh_out[...] = fresh

    base = jnp.zeros((rows, kv_width), F32)
    for c in range(pieces):
        weight_copy(c).wait()
        part = slice(c * tall, (c + 1) * tall)
        base = base + jnp.dot(hidden[:, part], weight_buf[part, :], preferred_element_type=F32)
    base_out[...] = base

    for g in range(groups):
        for c in range(CAP):

            @pl.when(counts[g] > c)
            def _():
                down_copy(0, g * CAP + c).wait()
                up_copy(0, g * CAP + c).wait()

    half = depth // 2
    width = low_out.shape[1]
    h_all = hidden_all[...].reshape(groups * 2 * rows, half)
    left = dot_nt(h_all, down_buf[:, :half])
    right = dot_nt(h_all, down_buf[:, half:])
    slot_lane = lax.broadcasted_iota(jnp.int32, (rows, width), 1) // ADAPTER_RANK
    slot_row = lax.broadcasted_iota(jnp.int32, (rows, width), 0)
    for g in range(groups):
        wanted = jnp.full((rows, width), -1, jnp.int32)
        for r in range(rows):
            wanted = jnp.where(slot_row == r, slots[g * entries + ids[g, r, 0]], wanted)
        top = g * 2 * rows
        low = left[top : top + rows] + right[top + rows : top + 2 * rows]
        low_out[g * rows : (g + 1) * rows] = jnp.where(wanted == slot_lane, low, 0.0)


def finish_kernel(
    groups,
    parts,
    low,
    up,
    base,
    acc,
    stats,
    fresh,
    value_out,
    attention_out,
    low_recv,
    base_recv,
    acc_recv,
    stats_recv,
    reply,
    reply_recv,
    value_heads,
    send_sems,
    recv_sems,
    reply_send,
    reply_recv_sems,
):
    me = lax.axis_index("req")
    tp = lax.axis_index("tp")
    rows, kv_width = base.shape
    kv_heads = kv_width // HD
    here = attention_out.shape[1] // HD
    per = here * parts // kv_heads
    columns = up.shape[1]
    total = groups * parts
    mine = me * parts + tp
    barrier = pltpu.get_barrier_semaphore()

    def member(o):
        at = lax.rem(mine + o, total)
        return at // parts, lax.rem(at, parts)

    def greet(o, _):
        peer_req, peer_tp = member(o)
        pl.semaphore_signal(
            barrier, inc=1, device_id={"req": peer_req, "tp": peer_tp}, device_id_type=MESH
        )
        return 0

    lax.fori_loop(1, total, greet, 0)
    low_recv[tp] = low[...]
    base_recv[tp] = base[...]
    stats_recv[tp] = stats[tp]
    acc_recv[tp] = acc[tp]
    pl.semaphore_wait(barrier, total - 1)

    def share(n, d):
        peer = lax.rem(tp + d, parts)
        source, landing = (
            lambda: (low, low_recv),
            lambda: (stats.at[peer], stats_recv),
            lambda: (base, base_recv),
            lambda: (acc.at[peer], acc_recv),
        )[n]()
        return pltpu.make_async_remote_copy(
            src_ref=source,
            dst_ref=landing.at[tp],
            send_sem=send_sems.at[n, d],
            recv_sem=recv_sems.at[n, d],
            device_id={"tp": peer},
            device_id_type=MESH,
        )

    def each(n, act):
        def step(d, _):
            act(share(n, d))
            return 0

        lax.fori_loop(1, parts, step, 0)

    for n in range(4):
        each(n, lambda copy: copy.start())
    each(0, lambda copy: copy.wait_recv())

    rank_sum = low_recv[0]
    for p in range(1, parts):
        rank_sum = rank_sum + low_recv[p]
    coarse = rank_sum.astype(BF16)
    fine = (rank_sum - coarse.astype(F32)).astype(BF16)
    term = jnp.dot(coarse, up[...], preferred_element_type=F32) + jnp.dot(
        fine, up[...], preferred_element_type=F32
    )
    for g in range(groups):
        reply[g] = term[g * rows : (g + 1) * rows]

    def reply_copy(o):
        peer_req, peer_tp = member(o)
        return pltpu.make_async_remote_copy(
            src_ref=reply.at[peer_req],
            dst_ref=reply_recv.at[me, tp],
            send_sem=reply_send.at[o],
            recv_sem=reply_recv_sems.at[o],
            device_id={"req": peer_req, "tp": peer_tp},
            device_id_type=MESH,
        )

    def reply_start(o, _):
        reply_copy(o).start()
        return 0

    lax.fori_loop(1, total, reply_start, 0)
    reply_recv[me, tp] = reply[me]

    for n in range(1, 4):
        each(n, lambda copy: copy.wait_recv())
    fresh_score = fresh[...]
    peak = fresh_score
    for p in range(parts):
        peak = jnp.maximum(peak, stats_recv[p, :rows])
    fresh_weight = jnp.exp(fresh_score - peak)
    weights = [jnp.exp(stats_recv[p, :rows] - peak) for p in range(parts)]
    den = fresh_weight
    for p in range(parts):
        den = den + weights[p] * stats_recv[p, rows:]
    inverse = 1.0 / den
    fresh_weight = fresh_weight * inverse
    weights = [weight * inverse for weight in weights]
    old = []
    for j in range(here):
        part = jnp.zeros((rows, HD), F32)
        for p in range(parts):
            block = acc_recv[p].astype(F32)[j * rows : (j + 1) * rows]
            part = part + weights[p][:, j : j + 1] * block
        old.append(part)

    base_sum = base_recv[0]
    for p in range(1, parts):
        base_sum = base_sum + base_recv[p]

    def reply_finish(o, _):
        reply_copy(o).wait_recv()
        return 0

    lax.fori_loop(1, total, reply_finish, 0)
    adapter = []
    for p in range(parts):
        piece = reply_recv[0, p]
        for g in range(1, groups):
            piece = piece + reply_recv[g, p]
        adapter.append(piece)
    value = (base_sum + jnp.concatenate(adapter, axis=1)).astype(BF16)
    value_out[...] = value
    value_f32 = value.astype(F32)
    for k in range(kv_heads):
        value_heads[k] = value_f32[:, k * HD : (k + 1) * HD]
    for j in range(here):
        fresh_value = value_heads[(tp * here + j) // per]
        out = old[j] + fresh_weight[:, j : j + 1] * fresh_value
        attention_out[:, j * HD : (j + 1) * HD] = out.astype(BF16)

    for n in range(4):
        each(n, lambda copy: copy.wait_send())

    def reply_sent(o, _):
        reply_copy(o).wait_send()
        return 0

    lax.fori_loop(1, total, reply_sent, 0)


def per_device(
    groups,
    parts,
    hidden,
    value_projection_weight,
    adapter_down_weight,
    adapter_up_weight,
    adapter_store_row,
    request_group_adapters,
    row_list_entry,
    cache_length,
    query,
    cached_key_rows,
    cached_value_rows,
    new_token_keys,
):
    rows, depth = hidden.shape
    kv_width = new_token_keys.shape[1]
    columns = adapter_up_weight.shape[2]
    heads = query.shape[1] // HD
    here = heads // parts
    block = cached_key_rows.shape[1]
    entries = request_group_adapters.shape[0]
    slot_rows = groups * CAP * ADAPTER_RANK
    total = groups * parts
    dma = pltpu.SemaphoreType.DMA
    shape = jax.ShapeDtypeStruct

    ids = jnp.concatenate([row_list_entry, request_group_adapters[:, None]], axis=1)
    ids = jnp.pad(ids, ((0, 0), (0, 126)))
    ids_all, hidden_all = pl.pallas_call(
        functools.partial(request_kernel, groups),
        out_shape=(
            shape((groups, entries, 128), jnp.int32),
            shape((groups, 2 * rows, depth // 2), BF16),
        ),
        in_specs=[VMEM] * 2,
        out_specs=(VMEM, VMEM),
        scratch_shapes=[dma((2, groups)), dma((2, groups))],
        compiler_params=pltpu.CompilerParams(collective_id=0, has_side_effects=True),
        name="request",
    )(ids, hidden)

    chunks = 4
    pieces = 4 if depth % 1024 == 0 else 1
    low, up, base, acc, stats, fresh = pl.pallas_call(
        functools.partial(local_kernel, groups, parts),
        out_shape=(
            shape((groups * rows, slot_rows), F32),
            shape((slot_rows, columns), BF16),
            shape((rows, kv_width), F32),
            shape((parts, here * rows, HD), BF16),
            shape((parts, 2 * rows, 128), F32),
            shape((rows, 128), F32),
        ),
        in_specs=[SMEM] * 3 + [VMEM] * 4 + [ANY] * 5,
        out_specs=(VMEM,) * 6,
        scratch_shapes=[
            pltpu.VMEM(cached_key_rows.shape, BF16),
            pltpu.VMEM(cached_value_rows.shape, BF16),
            pltpu.VMEM(value_projection_weight.shape, BF16),
            pltpu.VMEM((slot_rows, depth), BF16),
            pltpu.SMEM((groups * entries,), jnp.int32),
            dma((chunks,)),
            dma((chunks,)),
            dma((pieces,)),
            dma((groups * CAP,)),
            dma((groups * CAP,)),
        ],
        compiler_params=pltpu.CompilerParams(vmem_limit_bytes=32 * 1024 * 1024),
        name="local",
    )(
        ids_all,
        adapter_store_row,
        cache_length,
        hidden_all,
        hidden,
        query,
        new_token_keys,
        value_projection_weight,
        adapter_down_weight,
        adapter_up_weight,
        cached_key_rows,
        cached_value_rows,
    )

    return pl.pallas_call(
        functools.partial(finish_kernel, groups, parts),
        out_shape=(shape((rows, kv_width), BF16), shape((rows, here * HD), BF16)),
        in_specs=[VMEM] * 6,
        out_specs=(VMEM, VMEM),
        scratch_shapes=[
            pltpu.VMEM((parts, groups * rows, slot_rows), F32),
            pltpu.VMEM((parts, rows, kv_width), F32),
            pltpu.VMEM((parts, here * rows, HD), BF16),
            pltpu.VMEM((parts, 2 * rows, 128), F32),
            pltpu.VMEM((groups, rows, columns), F32),
            pltpu.VMEM((groups, parts, rows, columns), F32),
            pltpu.VMEM((kv_width // HD, rows, HD), F32),
            dma((4, parts)),
            dma((4, parts)),
            dma((total,)),
            dma((total,)),
        ],
        compiler_params=pltpu.CompilerParams(
            collective_id=1, has_side_effects=True, vmem_limit_bytes=32 * 1024 * 1024
        ),
        name="finish",
    )(low, up, base, acc, stats, fresh)


def solution(mesh):
    return jax.shard_map(
        functools.partial(per_device, mesh.shape["req"], mesh.shape["tp"]),
        mesh=mesh,
        in_specs=(
            P(("rep", "req"), "tp"),
            P("tp", None),
            P(("rep", "req"), None, "tp"),
            P(("rep", "req"), None, "tp"),
            P("rep"),
            P(("rep", "req")),
            P(("rep", "req"), None),
            P(("rep", "req")),
            P(("rep", "req"), None),
            P(("rep", "req"), "tp", None),
            P(("rep", "req"), "tp", None),
            P(("rep", "req"), None),
        ),
        out_specs=(P(("rep", "req"), None), P(("rep", "req"), "tp")),
        check_vma=False,
    )
```

time: 122 us -> 49.1 us (0.40)
  blocking collectives: 67.3 us -> 0 us
  Pallas kernels: 0 us -> 32.4 us
  between operations: 15 us -> 0.67 us
  matrix products: 8.97 us -> 0 us
  other arithmetic: 7.62 us -> 0.68 us
  starting transfers between devices: 6.8 us -> 0 us
  waiting for transfers between devices: 4.81 us -> 0 us
  local copies, waits for them, and re-layouts: 10.5 us -> 14.8 us
    all_gather x3 -> x0, blocking collectives: 41.1 us -> none  [the longest x2 27.9 us: joined(): everything = jax.tree.map(lambda part: lax.all_gather(part, axis), value)]
    pallas_call x0 -> x3, Pallas kernels: none -> 32.4 us  [the longest x1 18 us: per_device(): pl.pallas_call(functools.partial(finish_kernel, groups, parts), out_shape...]
    psum x1 -> x0, blocking collectives: 19.8 us -> none  [per_device(): value_sum, low_rank = lax.psum((base_part, low_part), 'tp')]
    unnamed x25 -> x24, local copies, waits for them, and re-layouts: 2.23 us -> 14.1 us
    dot_general x6 -> x0, matrix products: 8.97 us -> none  [the longest x1 2.84 us: per_device(): jnp.dot(hidden, value_projection_weight, preferred_element_type=jnp.float32)]
    all_to_all x2 -> x0, starting transfers between devices: 6.76 us -> none  [the longest x1 3.48 us: per_device(): lax.all_to_all(down_outgoing, 'req', split_axis=0, concat_axis=0, tiled=T...]
    unnamed x1 -> x0, blocking collectives: 6.35 us -> none
    gather x4 -> x0, local copies, waits for them, and re-layouts: 6.27 us -> none  [the longest x1 2.88 us: per_device(): adapter_up_weight[outgoing_slot]]
  transfers between devices with their start and end apart: 3 -> 0, of which waited for: 1 -> 0; matrix products, arithmetic and copies ran while one was open for 13% -> 0% of each run, Pallas kernels for 0% -> 0%
where the time goes in v1:
time: 49.1 us; the launch traced here: 48.6 us
  Pallas kernels  32.4 us (66%)
  local copies, waits for them, and re-layouts  14.8 us (30%)
  other arithmetic  0.68 us (1%)
  between operations  0.67 us (1%)
    pallas_call x1, Pallas kernels, per_device(): pl.pallas_call(functools.partial(finish_kernel, groups, parts), out_shape...  18 us
    unnamed x24, local copies, waits for them, and re-layouts  14.1 us
    pallas_call x1, Pallas kernels, per_device(): pl.pallas_call(functools.partial(local_kernel, groups, parts), out_shape=...  7.54 us
    pallas_call x1, Pallas kernels, per_device(): pl.pallas_call(functools.partial(request_kernel, groups), out_shape=(shap...  6.85 us

profile of v1, /device:TPU:0, one launch (start us, length us, event | category | flops | bytes accessed | tf_op | source)
XLA Modules:
  0.0 48.6 jit_solution(16043458515197881580)
XLA Ops:
  0.6 0.7 %pad_add_fusion = s32[8,2]{0,1:T(2,128)S(1)} fusion(s32[8,1]{0,1:T(1,128)} %bitcast.1, s32[8,1]{0,1:T(1,128)} %param.18), kind=kLoop, calls=%fused_computation | loop fusion | flops 16 | bytes 128 | tf_op jit(solution)/shard_map/concatenate | solution.py:467
  1.3 0.1 copy.16
  1.4 0.6 %pad.4.ids_ref = s32[8,128]{1,0:T(8,128)} pad(s32[8,2]{1,0:T(8,128)S(1)} %copy.16, s32[]{:T(128)} %constant.0.clone.1), padding=0_0x0_126 | pad | bytes 4164 | tf_op jit(solution)/shard_map/jit(_pad)/pad | solution.py:468
  2.0 6.9 %request.1 = (s32[4,8,128]{2,1,0:T(8,128)}, bf16[4,16,1024]{2,1,0:T(8,128)(2,1)}) custom-call(s32[8,128]{1,0:T(8,128)} %pad.4.ids_ref, bf16[8,2048]{1,0:T(8,128)(2,1)} %hidden.1), custom_call_target="tpu_custom_call" | custom-call | tf_op jit(solution)/shard_map/request/pallas_call | solution.py:469
  8.9 0.0 copy-start
  8.9 2.2 %copy-done = bf16[2048,1024]{1,0:T(8,128)(2,1)S(1)} copy-done((bf16[2048,1024]{1,0:T(8,128)(2,1)S(1)}, bf16[2048,1024]{1,0:T(8,128)(2,1)}, u32[]{:S(2)}) %copy-start) | copy-done | bytes 4194328
  11.0 0.0 copy-start.1
  11.0 2.2 %copy-done.1 = bf16[512,16,256]{2,1,0:T(8,128)(2,1)S(1)} copy-done((bf16[512,16,256]{2,1,0:T(8,128)(2,1)S(1)}, bf16[512,16,256]{2,1,0:T(8,128)(2,1)}, u32[]{:S(2)}) %copy-start.1) | copy-done | bytes 4194328
  13.2 0.0 copy-start.2
  13.2 1.6 %copy-done.2 = bf16[8,128,1024]{2,1,0:T(8,128)(2,1)S(1)} copy-done((bf16[8,128,1024]{2,1,0:T(8,128)(2,1)S(1)}, bf16[8,128,1024]{2,1,0:T(8,128)(2,1)}, u32[]{:S(2)}) %copy-start.2) | copy-done | bytes 2097176
  14.8 0.0 copy-start.3
  14.8 1.6 %copy-done.3 = bf16[8,128,1024]{2,1,0:T(8,128)(2,1)S(1)} copy-done((bf16[8,128,1024]{2,1,0:T(8,128)(2,1)S(1)}, bf16[8,128,1024]{2,1,0:T(8,128)(2,1)}, u32[]{:S(2)}) %copy-start.3) | copy-done | bytes 2097176
  16.4 0.0 copy-start.4
  16.4 0.9 %copy-done.4 = bf16[8,8192]{1,0:T(8,128)(2,1)S(1)} copy-done((bf16[8,8192]{1,0:T(8,128)(2,1)S(1)}, bf16[8,8192]{1,0:T(8,128)(2,1)}, u32[]{:S(2)}) %copy-start.4) | copy-done | bytes 131096
  17.3 0.9 %copy-done.5 = bf16[4,16,1024]{2,1,0:T(8,128)(2,1)S(1)} copy-done((bf16[4,16,1024]{2,1,0:T(8,128)(2,1)S(1)}, bf16[4,16,1024]{2,1,0:T(8,128)(2,1)}, u32[]{:S(2)}) %copy-start.5) | copy-done | bytes 131096
  18.2 0.8 %copy-done.6 = bf16[8,2048]{1,0:T(8,128)(2,1)S(1)} copy-done((bf16[8,2048]{1,0:T(8,128)(2,1)S(1)}, bf16[8,2048]{1,0:T(8,128)(2,1)}, u32[]{:S(2)}) %copy-start.6) | copy-done | bytes 32792
  19.0 0.7 %copy-done.7 = bf16[8,1024]{1,0:T(8,128)(2,1)S(1)} copy-done((bf16[8,1024]{1,0:T(8,128)(2,1)S(1)}, bf16[8,1024]{1,0:T(8,128)(2,1)}, u32[]{:S(2)}) %copy-start.7) | copy-done | bytes 16408
  19.7 0.7 %copy-done.8 = s32[4,8,128]{2,1,0:T(8,128)S(1)} copy-done((s32[4,8,128]{2,1,0:T(8,128)S(1)}, s32[4,8,128]{2,1,0:T(8,128)}, u32[]{:S(2)}) %copy-start.8) | copy-done | bytes 16408
  20.4 0.7 %copy-done.9 = s32[2048]{0:T(1024)S(1)} copy-done((s32[2048]{0:T(1024)S(1)}, s32[2048]{0:T(1024)}, u32[]{:S(2)}) %copy-start.9) | copy-done | bytes 8216
  21.1 0.7 %copy-done.10 = s32[8]{0:T(128)S(1)} copy-done((s32[8]{0:T(128)S(1)}, s32[8]{0:T(128)}, u32[]{:S(2)}) %copy-start.10) | copy-done | bytes 56
  21.8 7.5 %local.1 = (f32[32,128]{1,0:T(8,128)S(1)}, bf16[128,256]{1,0:T(8,128)(2,1)S(1)}, f32[8,1024]{1,0:T(8,128)S(1)}, bf16[4,128,128]{2,1,0:T(8,128)(2,1)S(1)}, f32[4,...) custom-call(s32[4,8,128]{2,1,0:T(8,128)S(1)} %copy-done.8, s32[2048]{0:T(1024)S(1)} %copy-done.9, s32[8]{0:T(128)S(1)} %copy-done.10, ...), custom_call_target="tpu_custom_call" | custom-call | tf_op jit(solution)/shard_map/local/pallas_call | solution.py:484
  29.3 18.0 %finish.1 = (bf16[8,1024]{1,0:T(8,128)(2,1)S(1)}, bf16[8,2048]{1,0:T(8,128)(2,1)S(1)}) custom-call(f32[32,128]{1,0:T(8,128)S(1)} %get-tuple-element.12.low, bf16[128,256]{1,0:T(8,128)(2,1)S(1)} %get-tuple-element.13.up, f32[8,1024]{1,0:T(8,128)S(1)} %get-tuple-element.14.base, bf16[4,128,128]{2,1,0:T(8,128)(2,1)S(1)} %get-tuple-element.15.acc, ...), custom_call_target="tpu_custom_call" | custom-call | tf_op jit(solution)/shard_map/finish/pallas_call | solution.py:525
  47.3 0.6 %copy.19 = bf16[8,1024]{1,0:T(8,128)(2,1)} copy(bf16[8,1024]{1,0:T(8,128)(2,1)S(1)} %get-tuple-element.20) | data formatting | bytes 32768
  47.9 0.6 %copy.20 = bf16[8,2048]{1,0:T(8,128)(2,1)} copy(bf16[8,2048]{1,0:T(8,128)(2,1)S(1)} %get-tuple-element.21) | data formatting | bytes 65536
  (6 shorter events, 0.0 us)
Async XLA Ops:
  8.9 2.2 %copy-start = (bf16[2048,1024]{1,0:T(8,128)(2,1)S(1)}, bf16[2048,1024]{1,0:T(8,128)(2,1)}, u32[]{:S(2)}) copy-start(bf16[2048,1024]{1,0:T(8,128)(2,1)} %weight.1) | copy-start | bytes 12582916
  11.0 2.2 %copy-start.1 = (bf16[512,16,256]{2,1,0:T(8,128)(2,1)S(1)}, bf16[512,16,256]{2,1,0:T(8,128)(2,1)}, u32[]{:S(2)}) copy-start(bf16[512,16,256]{2,1,0:T(8,128)(2,1)} %up.1) | copy-start | bytes 12582916
  13.2 1.6 %copy-start.2 = (bf16[8,128,1024]{2,1,0:T(8,128)(2,1)S(1)}, bf16[8,128,1024]{2,1,0:T(8,128)(2,1)}, u32[]{:S(2)}) copy-start(bf16[8,128,1024]{2,1,0:T(8,128)(2,1)} %keys.1) | copy-start | bytes 6291460
  14.8 1.6 %copy-start.3 = (bf16[8,128,1024]{2,1,0:T(8,128)(2,1)S(1)}, bf16[8,128,1024]{2,1,0:T(8,128)(2,1)}, u32[]{:S(2)}) copy-start(bf16[8,128,1024]{2,1,0:T(8,128)(2,1)} %values.1) | copy-start | bytes 6291460
  16.4 0.9 %copy-start.4 = (bf16[8,8192]{1,0:T(8,128)(2,1)S(1)}, bf16[8,8192]{1,0:T(8,128)(2,1)}, u32[]{:S(2)}) copy-start(bf16[8,8192]{1,0:T(8,128)(2,1)} %query.1) | copy-start | bytes 393220
  17.3 0.9 %copy-start.5 = (bf16[4,16,1024]{2,1,0:T(8,128)(2,1)S(1)}, bf16[4,16,1024]{2,1,0:T(8,128)(2,1)}, u32[]{:S(2)}) copy-start(bf16[4,16,1024]{2,1,0:T(8,128)(2,1)} %get-tuple-element.11.hidden_all) | copy-start | bytes 393220
  18.2 0.8 %copy-start.6 = (bf16[8,2048]{1,0:T(8,128)(2,1)S(1)}, bf16[8,2048]{1,0:T(8,128)(2,1)}, u32[]{:S(2)}) copy-start(bf16[8,2048]{1,0:T(8,128)(2,1)} %hidden.1) | copy-start | bytes 98308
  19.0 0.7 %copy-start.7 = (bf16[8,1024]{1,0:T(8,128)(2,1)S(1)}, bf16[8,1024]{1,0:T(8,128)(2,1)}, u32[]{:S(2)}) copy-start(bf16[8,1024]{1,0:T(8,128)(2,1)} %new_keys.1) | copy-start | bytes 49156
  19.7 0.7 %copy-start.8 = (s32[4,8,128]{2,1,0:T(8,128)S(1)}, s32[4,8,128]{2,1,0:T(8,128)}, u32[]{:S(2)}) copy-start(s32[4,8,128]{2,1,0:T(8,128)} %get-tuple-element.10.ids) | copy-start | bytes 49156
  20.4 0.7 %copy-start.9 = (s32[2048]{0:T(1024)S(1)}, s32[2048]{0:T(1024)}, u32[]{:S(2)}) copy-start(s32[2048]{0:T(1024)} %table.1) | copy-start | bytes 24580
  21.1 0.7 %copy-start.10 = (s32[8]{0:T(128)S(1)}, s32[8]{0:T(128)}, u32[]{:S(2)}) copy-start(s32[8]{0:T(128)} %lengths.1) | copy-start | bytes 100

commit v2 on v1

v2 whole, which is shorter than its diff:
```python
import functools

import jax
import jax.numpy as jnp
from jax import lax
from jax.experimental import pallas as pl
from jax.experimental.pallas import tpu as pltpu
from jax.sharding import PartitionSpec as P

HD = 128
ADAPTER_RANK = 16
CAP = 2
MASKED = -1e30
F32 = jnp.float32
BF16 = jnp.bfloat16
MESH = pl.DeviceIdType.MESH
VMEM = pl.BlockSpec(memory_space=pltpu.VMEM)
HBM = pl.BlockSpec(memory_space=pltpu.HBM)
ANY = pl.BlockSpec(memory_space=pl.ANY)
ROOM = 48 * 1024 * 1024


def dot_nt(a, b):
    return lax.dot_general(a, b, (((1,), (1,)), ((), ())), preferred_element_type=F32)


def repeated(x):
    for step in (16, 32, 64):
        x = x + pltpu.roll(x, step, axis=1)
    return x


def attend_kernel(
    groups,
    parts,
    wanted,
    picks,
    lengths,
    hidden,
    query,
    new_keys,
    keys,
    values,
    ids_out,
    hidden_out,
    acc_out,
    stats_out,
    fresh_out,
    wanted_s,
    picks_s,
    lengths_s,
    hidden_v,
    query_v,
    new_keys_v,
    key_buf,
    value_buf,
    acc_send,
    stats_send,
    small_sems,
    key_sems,
    value_sems,
    req_send,
    req_recv,
    tp_send,
    tp_recv,
):
    me = lax.axis_index("req")
    tp = lax.axis_index("tp")
    rows, depth = hidden.shape
    kv_width = new_keys.shape[1]
    kv_heads = kv_width // HD
    heads = query.shape[1] // HD
    per = heads // kv_heads
    here = heads // parts
    block = keys.shape[1]
    scale = HD ** (-0.5)
    half = depth // 2
    chunks = key_sems.shape[0]
    wide = kv_width // chunks
    inner = chunks == parts
    barrier = pltpu.get_barrier_semaphore()

    def greet_req(d, _):
        peer = lax.rem(me + d, groups)
        pl.semaphore_signal(barrier, inc=1, device_id={"req": peer}, device_id_type=MESH)
        return 0

    def greet_tp(d, _):
        peer = lax.rem(tp + d, parts)
        pl.semaphore_signal(barrier, inc=1, device_id={"tp": peer}, device_id_type=MESH)
        return 0

    lax.fori_loop(1, groups, greet_req, 0)
    lax.fori_loop(1, parts, greet_tp, 0)

    small = [
        pltpu.make_async_copy(source, landing, small_sems.at[n])
        for n, (source, landing) in enumerate(
            (
                (wanted, wanted_s),
                (picks, picks_s),
                (hidden, hidden_v),
                (lengths, lengths_s),
                (query, query_v),
                (new_keys, new_keys_v),
            )
        )
    ]
    for copy in small:
        copy.start()

    def cache_copies(d):
        chunk = lax.rem(tp + d, chunks) if inner else d
        part = pl.ds(pl.multiple_of(chunk * wide, HD), wide)
        return [
            pltpu.make_async_copy(source.at[:, :, part], landing.at[:, :, part], sems.at[chunk])
            for source, landing, sems in ((keys, key_buf, key_sems), (values, value_buf, value_sems))
        ]

    for d in range(1, chunks + 1):
        for copy in cache_copies(d if inner else d - 1):
            copy.start()

    for copy in small[:3]:
        copy.wait()
    wide_rows = hidden_v[...].astype(F32)
    hidden_out[me] = jnp.concatenate([wide_rows[:, :half], wide_rows[:, half:]], axis=0).astype(
        BF16
    )
    entries = wanted_s.shape[0]
    lane = lax.broadcasted_iota(jnp.int32, (entries, 128), 1)
    sub = lax.broadcasted_iota(jnp.int32, (entries, 128), 0)
    ids = jnp.zeros((entries, 128), jnp.int32)
    for e in range(entries):
        ids = jnp.where(sub == e, jnp.where(lane == 0, picks_s[e], wanted_s[e]), ids)
    ids_out[me] = ids
    pl.semaphore_wait(barrier, groups + parts - 2)

    def request(n, d):
        peer = lax.rem(me + d, groups)
        ref = (ids_out, hidden_out)[n]
        return pltpu.make_async_remote_copy(
            src_ref=ref.at[me],
            dst_ref=ref.at[me],
            send_sem=req_send.at[n, d],
            recv_sem=req_recv.at[n, d],
            device_id={"req": peer},
            device_id_type=MESH,
        )

    def share(n, d):
        peer = lax.rem(tp + d, parts)
        source, landing = ((acc_send, acc_out), (stats_send, stats_out))[n]
        return pltpu.make_async_remote_copy(
            src_ref=source.at[peer],
            dst_ref=landing.at[tp],
            send_sem=tp_send.at[n, d],
            recv_sem=tp_recv.at[n, d],
            device_id={"tp": peer},
            device_id_type=MESH,
        )

    def request_start(d, _):
        for n in range(2):
            request(n, d).start()
        return 0

    def request_wait(d, _):
        for n in range(2):
            request(n, d).wait()
        return 0

    def share_wait(d, _):
        for n in range(2):
            share(n, d).wait()
        return 0

    lax.fori_loop(1, groups, request_start, 0)
    for copy in small[3:]:
        copy.wait()

    count = min(per, here)
    spans = here // count
    tall = count * rows
    sub_b = lax.broadcasted_iota(jnp.int32, (rows, block), 0)
    length = jnp.zeros((rows, block), jnp.int32)
    for r in range(rows):
        length = jnp.where(sub_b == r, lengths_s[r], length)
    position = tp * block + lax.broadcasted_iota(jnp.int32, (rows, block), 1)
    valid = jnp.concatenate([(position < length).astype(jnp.int32)] * count, axis=0) > 0

    def own_row(width):
        row = lax.rem(lax.broadcasted_iota(jnp.int32, (tall, rows * width), 0), rows)
        col = lax.broadcasted_iota(jnp.int32, (tall, rows * width), 1) // width
        return jnp.where(row == col, 1.0, 0.0).astype(BF16)

    own_key = own_row(HD)
    lined = block % 128 == 0
    own_prob = own_key if block == HD else own_row(block) if lined else None
    row_of = lax.rem(lax.broadcasted_iota(jnp.int32, (tall, block), 0), rows)
    lane = lax.broadcasted_iota(jnp.int32, (rows, 128), 1)

    def columns(first):
        return pl.ds(pl.multiple_of(first * HD, HD), HD)

    def attend(d):
        peer = lax.rem(tp + d, parts)
        if inner:
            for copy in cache_copies(d):
                copy.wait()
        stats = jnp.zeros((rows, 128), F32)
        for i in range(spans):
            first = peer * here + i * count
            cols = columns(first // per)
            q = jnp.concatenate(
                [query_v[:, columns(first + g)].astype(F32) for g in range(count)], axis=0
            ).astype(BF16)
            q_wide = jnp.concatenate([q] * rows, axis=1) * own_key
            k_wide = jnp.concatenate([key_buf[r, :, cols] for r in range(rows)], axis=1)
            score = dot_nt(q_wide, k_wide) * scale
            score = jnp.where(valid, score, MASKED)
            peak = jnp.max(score, axis=1, keepdims=True)
            prob = jnp.where(valid, jnp.exp(score - peak), 0.0).astype(BF16)
            prob_f32 = prob.astype(F32)
            total = jnp.sum(prob_f32, axis=1, keepdims=True)
            if lined:
                p_wide = jnp.concatenate([prob] * rows, axis=1) * own_prob
                v_tall = value_buf[:, :, cols].reshape(rows * block, HD)
                acc = jnp.dot(p_wide, v_tall, preferred_element_type=F32)
            else:
                acc = jnp.zeros((tall, HD), F32)
                for r in range(rows):
                    p_row = jnp.where(row_of == r, prob_f32, 0.0).astype(BF16)
                    acc = acc + jnp.dot(p_row, value_buf[r, :, cols], preferred_element_type=F32)
            acc_send[peer, i * tall : (i + 1) * tall, :] = acc.astype(BF16)
            for g in range(count):
                part = slice(g * rows, (g + 1) * rows)
                stats = jnp.where(lane == i * count + g, peak[part], stats)
                stats = jnp.where(lane == 64 + i * count + g, total[part], stats)
        stats_send[peer] = stats

    if not inner:
        for d in range(chunks):
            for copy in cache_copies(d):
                copy.wait()

    def step(d, _):
        attend(d)
        for n in range(2):
            share(n, d).start()
        return 0

    lax.fori_loop(1, parts, step, 0)
    attend(parts)
    acc_out[tp] = acc_send[tp]
    stats_out[tp] = stats_send[tp]

    fresh = jnp.zeros((rows, 128), F32)
    for j in range(here):
        head = tp * here + j
        both = query_v[:, columns(head)].astype(F32) * new_keys_v[:, columns(head // per)].astype(
            F32
        )
        fresh = jnp.where(lane == j, jnp.sum(both, axis=1, keepdims=True) * scale, fresh)
    fresh_out[...] = fresh
    lax.fori_loop(1, groups, request_wait, 0)
    lax.fori_loop(1, parts, share_wait, 0)


def adapter_kernel(
    groups,
    parts,
    ids_in,
    hidden_all,
    table_in,
    weight,
    down,
    up,
    low_out,
    up_out,
    base_out,
    mask_out,
    ids,
    table,
    weight_buf,
    down_buf,
    slots,
    small_sems,
    weight_sems,
    down_sems,
    up_sems,
):
    me = lax.axis_index("req")
    depth, kv_width = weight.shape
    rows = hidden_all.shape[1] // 2
    store = down.shape[0]
    entries = ids.shape[1]
    columns = up.shape[2]
    half = depth // 2
    pieces = weight_sems.shape[0]
    tall = depth // pieces
    width = mask_out.shape[1]

    small = [
        pltpu.make_async_copy(ids_in, ids, small_sems.at[0]),
        pltpu.make_async_copy(table_in, table, small_sems.at[1]),
    ]

    def weight_copy(c):
        part = pl.ds(c * tall, tall)
        return pltpu.make_async_copy(weight.at[part, :], weight_buf.at[part, :], weight_sems.at[c])

    def down_copy(place, slot):
        part = pl.ds(slot * ADAPTER_RANK, ADAPTER_RANK)
        return pltpu.make_async_copy(down.at[place], down_buf.at[part, :], down_sems.at[slot])

    def up_copy(place, slot):
        part = pl.ds(lax.rem(slot, CAP) * ADAPTER_RANK, ADAPTER_RANK)
        return pltpu.make_async_copy(
            up.at[place], up_out.at[slot // CAP, part, :], up_sems.at[slot]
        )

    for copy in small:
        copy.start()
    for c in range(pieces):
        weight_copy(c).start()
    up_out[...] = jnp.zeros_like(up_out)
    for copy in small:
        copy.wait()

    counts = []
    for g in range(groups):
        count = jnp.int32(0)
        for e in range(entries):
            at = table[ids[g, e, 1]]
            mine = (at // store == me) & (count < CAP)
            slot = g * CAP + count
            slots[g * entries + e] = jnp.where(mine, slot, -1)

            @pl.when(mine)
            def _():
                down_copy(lax.rem(at, store), slot).start()
                up_copy(lax.rem(at, store), slot).start()

            count = count + mine.astype(jnp.int32)
        counts.append(count)

    owners = [table[ids[me, e, 1]] // store for e in range(entries)]
    for e in range(entries):
        order = jnp.int32(0)
        for before in range(e):
            order = order + (owners[before] == owners[e]).astype(jnp.int32)
        slots[groups * entries + e] = owners[e] * CAP + order
    slot_lane = lax.broadcasted_iota(jnp.int32, (rows, width), 1) // ADAPTER_RANK
    slot_row = lax.broadcasted_iota(jnp.int32, (rows, width), 0)
    place = jnp.full((rows, width), -1, jnp.int32)
    for r in range(rows):
        place = jnp.where(slot_row == r, slots[groups * entries + ids[me, r, 0]], place)
    mask_out[...] = jnp.where(place == slot_lane, 1.0, 0.0)

    own = hidden_all[me]
    base = [jnp.zeros((2 * rows, kv_width), F32) for _ in range(2)]
    for c in range(pieces):
        weight_copy(c).wait()
        side, at = divmod(c * tall, half)
        base[side] = base[side] + jnp.dot(
            own[:, at : at + tall], weight_buf[c * tall : (c + 1) * tall, :],
            preferred_element_type=F32,
        )
    both = base[0][:rows] + base[1][rows:]
    for p in range(parts):
        base_out[p] = both[:, p * columns : (p + 1) * columns]

    for g in range(groups):
        for c in range(CAP):

            @pl.when(counts[g] > c)
            def _():
                down_copy(0, g * CAP + c).wait()
                up_copy(0, g * CAP + c).wait()

    h_all = hidden_all[...].reshape(groups * 2 * rows, half)
    left = dot_nt(h_all, down_buf[:, :half])
    right = dot_nt(h_all, down_buf[:, half:])
    lane = lax.broadcasted_iota(jnp.int32, (rows, 128), 1) // ADAPTER_RANK
    sub = lax.broadcasted_iota(jnp.int32, (rows, 128), 0)
    for g in range(groups):
        wanted = jnp.full((rows, width), -1, jnp.int32)
        for r in range(rows):
            wanted = jnp.where(slot_row == r, slots[g * entries + ids[g, r, 0]], wanted)
        top = g * 2 * rows
        low = left[top : top + rows] + right[top + rows : top + 2 * rows]
        low = jnp.where(wanted == slot_lane, low, 0.0)
        folded = low[:, :128]
        for c in range(1, width // 128):
            folded = folded + low[:, c * 128 : (c + 1) * 128]
        low_out[g] = jnp.sum(
            jnp.where(lane == sub, repeated(folded), 0.0), axis=0, keepdims=True
        )


def finish_kernel(
    groups,
    parts,
    low,
    up,
    base,
    mask,
    acc,
    stats,
    fresh,
    value_out,
    attention_out,
    low_recv,
    up_recv,
    base_recv,
    value_recv,
    value_heads,
    low_send_sems,
    low_recv_sems,
    up_send_sems,
    up_recv_sems,
    tp_send_sems,
    tp_recv_sems,
):
    me = lax.axis_index("req")
    tp = lax.axis_index("tp")
    rows, kv_width = value_out.shape
    kv_heads = kv_width // HD
    here = attention_out.shape[1] // HD
    per = here * parts // kv_heads
    columns = up.shape[2]
    width = mask.shape[1]
    total = groups * parts
    mine = me * parts + tp
    barrier = pltpu.get_barrier_semaphore()

    def member(o):
        at = lax.rem(mine + o, total)
        return {"req": at // parts, "tp": lax.rem(at, parts)}

    def greet(o, _):
        pl.semaphore_signal(barrier, inc=1, device_id=member(o), device_id_type=MESH)
        return 0

    lax.fori_loop(1, total, greet, 0)
    low_recv[mine] = low[me]
    up_recv[me] = up[me]
    base_recv[tp] = base[tp]

    def low_copy(o):
        peer = member(o)
        return pltpu.make_async_remote_copy(
            src_ref=low.at[peer["req"]],
            dst_ref=low_recv.at[mine],
            send_sem=low_send_sems.at[o],
            recv_sem=low_recv_sems.at[o],
            device_id=peer,
            device_id_type=MESH,
        )

    def up_copy(d):
        peer = lax.rem(me + d, groups)
        return pltpu.make_async_remote_copy(
            src_ref=up.at[peer],
            dst_ref=up_recv.at[me],
            send_sem=up_send_sems.at[d],
            recv_sem=up_recv_sems.at[d],
            device_id={"req": peer},
            device_id_type=MESH,
        )

    def tp_copy(n, d):
        peer = lax.rem(tp + d, parts)
        source = value_recv.at[tp] if n else base.at[peer]
        landing = value_recv if n else base_recv
        return pltpu.make_async_remote_copy(
            src_ref=source,
            dst_ref=landing.at[tp],
            send_sem=tp_send_sems.at[n, d],
            recv_sem=tp_recv_sems.at[n, d],
            device_id={"tp": peer},
            device_id_type=MESH,
        )

    def each(count, act):
        def step(d, _):
            act(d)
            return 0

        lax.fori_loop(1, count, step, 0)

    pl.semaphore_wait(barrier, total - 1)
    each(parts, lambda d: tp_copy(0, d).start())
    each(groups, lambda d: up_copy(d).start())
    each(total, lambda o: low_copy(o).start())

    fresh_score = fresh[...]
    peak = fresh_score
    for p in range(parts):
        peak = jnp.maximum(peak, stats[p])
    fresh_weight = jnp.exp(fresh_score - peak)
    den = fresh_weight
    weights = []
    for p in range(parts):
        weight = jnp.exp(stats[p] - peak)
        den = den + weight * pltpu.roll(stats[p], 64, axis=1)
        weights.append(weight)
    inverse = 1.0 / den
    fresh_weight = fresh_weight * inverse
    weights = [weight * inverse for weight in weights]
    old = []
    for j in range(here):
        if (j * rows) % 16 == 0:
            pair = [acc[p, j * rows : (j + 2) * rows, :].astype(F32) for p in range(parts)]
        at = (j * rows) % 16
        part = jnp.zeros((rows, HD), F32)
        for p in range(parts):
            part = part + weights[p][:, j : j + 1] * pair[p][at : at + rows]
        old.append(part)

    each(parts, lambda d: tp_copy(0, d).wait_recv())
    base_sum = base_recv[0]
    for p in range(1, parts):
        base_sum = base_sum + base_recv[p]
    each(total, lambda o: low_copy(o).wait_recv())
    each(groups, lambda d: up_copy(d).wait_recv())
    rank_sum = jnp.sum(low_recv[...].reshape(total, 128), axis=0, keepdims=True)
    lane = lax.broadcasted_iota(jnp.int32, (rows, 128), 1) // ADAPTER_RANK
    sub = lax.broadcasted_iota(jnp.int32, (rows, 128), 0)
    by_row = repeated(jnp.where(lane == sub, jnp.broadcast_to(rank_sum, (rows, 128)), 0.0))
    low_rank = jnp.concatenate([by_row] * (width // 128), axis=1) * mask[...]
    coarse = low_rank.astype(BF16)
    fine = (low_rank - coarse.astype(F32)).astype(BF16)
    matrices = up_recv[...].reshape(width, columns)
    term = jnp.dot(coarse, matrices, preferred_element_type=F32) + jnp.dot(
        fine, matrices, preferred_element_type=F32
    )
    value_recv[tp] = (base_sum + term).astype(BF16).astype(F32)
    each(parts, lambda d: tp_copy(1, d).start())
    each(total, lambda o: low_copy(o).wait_send())
    each(groups, lambda d: up_copy(d).wait_send())
    each(parts, lambda d: tp_copy(0, d).wait_send())
    each(parts, lambda d: tp_copy(1, d).wait_recv())
    value = jnp.concatenate([value_recv[p] for p in range(parts)], axis=1)
    value_out[...] = value.astype(BF16)
    for k in range(kv_heads):
        value_heads[k] = value[:, k * HD : (k + 1) * HD]
    for j in range(here):
        fresh_value = value_heads[(tp * here + j) // per]
        out = old[j] + fresh_weight[:, j : j + 1] * fresh_value
        attention_out[:, j * HD : (j + 1) * HD] = out.astype(BF16)
    each(parts, lambda d: tp_copy(1, d).wait_send())


def per_device(
    groups,
    parts,
    hidden,
    value_projection_weight,
    adapter_down_weight,
    adapter_up_weight,
    adapter_store_row,
    request_group_adapters,
    row_list_entry,
    cache_length,
    query,
    cached_key_rows,
    cached_value_rows,
    new_token_keys,
):
    rows, depth = hidden.shape
    kv_width = new_token_keys.shape[1]
    kv_heads = kv_width // HD
    columns = adapter_up_weight.shape[2]
    heads = query.shape[1] // HD
    here = heads // parts
    entries = request_group_adapters.shape[0]
    slot_rows = groups * CAP * ADAPTER_RANK
    total = groups * parts
    chunks = min(parts, kv_heads)
    dma = pltpu.SemaphoreType.DMA
    shape = jax.ShapeDtypeStruct

    ids_all, hidden_all, acc, stats, fresh = pl.pallas_call(
        functools.partial(attend_kernel, groups, parts),
        out_shape=(
            shape((groups, entries, 128), jnp.int32),
            shape((groups, 2 * rows, depth // 2), BF16),
            shape((parts, here * rows, HD), BF16),
            shape((parts, rows, 128), F32),
            shape((rows, 128), F32),
        ),
        in_specs=[HBM] * 8,
        out_specs=(VMEM,) * 5,
        scratch_shapes=[
            pltpu.SMEM((entries,), jnp.int32),
            pltpu.SMEM((rows,), jnp.int32),
            pltpu.SMEM((rows,), jnp.int32),
            pltpu.VMEM(hidden.shape, BF16),
            pltpu.VMEM(query.shape, BF16),
            pltpu.VMEM(new_token_keys.shape, BF16),
            pltpu.VMEM(cached_key_rows.shape, BF16),
            pltpu.VMEM(cached_value_rows.shape, BF16),
            pltpu.VMEM((parts, here * rows, HD), BF16),
            pltpu.VMEM((parts, rows, 128), F32),
            dma((6,)),
            dma((chunks,)),
            dma((chunks,)),
            dma((2, groups)),
            dma((2, groups)),
            dma((2, parts)),
            dma((2, parts)),
        ],
        compiler_params=pltpu.CompilerParams(
            collective_id=0, has_side_effects=True, vmem_limit_bytes=ROOM
        ),
        name="attend",
    )(
        request_group_adapters,
        row_list_entry.reshape(rows),
        cache_length,
        hidden,
        query,
        new_token_keys,
        cached_key_rows,
        cached_value_rows,
    )

    pieces = 4 if depth % 1024 == 0 else 2
    low, up, base, mask = pl.pallas_call(
        functools.partial(adapter_kernel, groups, parts),
        out_shape=(
            shape((groups, 1, 128), F32),
            shape((groups, CAP * ADAPTER_RANK, columns), BF16),
            shape((parts, rows, columns), F32),
            shape((rows, slot_rows), F32),
        ),
        in_specs=[ANY, VMEM] + [HBM] * 4,
        out_specs=(VMEM,) * 4,
        scratch_shapes=[
            pltpu.SMEM((groups, entries, 128), jnp.int32),
            pltpu.SMEM(adapter_store_row.shape, jnp.int32),
            pltpu.VMEM(value_projection_weight.shape, BF16),
            pltpu.VMEM((slot_rows, depth), BF16),
            pltpu.SMEM(((groups + 1) * entries,), jnp.int32),
            dma((2,)),
            dma((pieces,)),
            dma((groups * CAP,)),
            dma((groups * CAP,)),
        ],
        compiler_params=pltpu.CompilerParams(vmem_limit_bytes=ROOM),
        name="adapters",
    )(
        ids_all,
        hidden_all,
        adapter_store_row,
        value_projection_weight,
        adapter_down_weight,
        adapter_up_weight,
    )

    return pl.pallas_call(
        functools.partial(finish_kernel, groups, parts),
        out_shape=(shape((rows, kv_width), BF16), shape((rows, here * HD), BF16)),
        in_specs=[VMEM] * 7,
        out_specs=(VMEM, VMEM),
        scratch_shapes=[
            pltpu.VMEM((total, 1, 128), F32),
            pltpu.VMEM((groups, CAP * ADAPTER_RANK, columns), BF16),
            pltpu.VMEM((parts, rows, columns), F32),
            pltpu.VMEM((parts, rows, columns), F32),
            pltpu.VMEM((kv_heads, rows, HD), F32),
            dma((total,)),
            dma((total,)),
            dma((groups,)),
            dma((groups,)),
            dma((2, parts)),
            dma((2, parts)),
        ],
        compiler_params=pltpu.CompilerParams(
            collective_id=1, has_side_effects=True, vmem_limit_bytes=ROOM
        ),
        name="finish",
    )(low, up, base, mask, acc, stats, fresh)


def solution(mesh):
    return jax.shard_map(
        functools.partial(per_device, mesh.shape["req"], mesh.shape["tp"]),
        mesh=mesh,
        in_specs=(
            P(("rep", "req"), "tp"),
            P("tp", None),
            P(("rep", "req"), None, "tp"),
            P(("rep", "req"), None, "tp"),
            P("rep"),
            P(("rep", "req")),
            P(("rep", "req"), None),
            P(("rep", "req")),
            P(("rep", "req"), None),
            P(("rep", "req"), "tp", None),
            P(("rep", "req"), "tp", None),
            P(("rep", "req"), None),
        ),
        out_specs=(P(("rep", "req"), None), P(("rep", "req"), "tp")),
        check_vma=False,
    )
```

time: 49.1 us -> 36.8 us (0.75)
  local copies, waits for them, and re-layouts: 14.8 us -> 9.04 us
  Pallas kernels: 32.4 us -> 26.7 us
  other arithmetic: 0.68 us -> 0 us
    pallas_call x1, Pallas kernels: 18 us -> 12.2 us  [per_device(): pl.pallas_call(functools.partial(finish_kernel, groups, parts), out_shape...]
    unnamed x24 -> x22, local copies, waits for them, and re-layouts: 14.1 us -> 9.04 us
    concatenate x1 -> x0, other arithmetic: 0.68 us -> none  [per_device(): jnp.concatenate([row_list_entry, request_group_adapters[:, None]], axis=1)]
    pad x1 -> x0, local copies, waits for them, and re-layouts: 0.6 us -> none  [per_device(): ids = jnp.pad(ids, ((0, 0), (0, 126)))]
where the time goes in v2:
time: 36.8 us; the launch traced here: 36.5 us
  Pallas kernels  26.7 us (73%)
  local copies, waits for them, and re-layouts  9.04 us (25%)
  between operations  0.7 us (2%)
    pallas_call x1, Pallas kernels, per_device(): pl.pallas_call(functools.partial(finish_kernel, groups, parts), out_shape...  12.2 us
    pallas_call x1, Pallas kernels, per_device(): pl.pallas_call(functools.partial(attend_kernel, groups, parts), out_shape...  11.5 us
    unnamed x22, local copies, waits for them, and re-layouts  9.04 us
    pallas_call x1, Pallas kernels, per_device(): pl.pallas_call(functools.partial(adapter_kernel, groups, parts), out_shap...  3.14 us

profile of v2, /device:TPU:0, one launch (start us, length us, event | category | flops | bytes accessed | tf_op | source)
XLA Modules:
  0.0 36.5 jit_solution(341972032901949440)
XLA Ops:
  0.6 0.0 copy-start
  0.6 0.0 copy-start.1
  0.7 1.7 %copy-done.1 = bf16[8,128,1024]{2,1,0:T(8,128)(2,1)S(1)} copy-done((bf16[8,128,1024]{2,1,0:T(8,128)(2,1)S(1)}, bf16[8,128,1024]{2,1,0:T(8,128)(2,1)}, u32[]{:S(2)}) %copy-start.1) | copy-done | bytes 2097176
  2.4 0.0 copy-start.2
  2.4 1.7 %copy-done.2 = bf16[8,128,1024]{2,1,0:T(8,128)(2,1)S(1)} copy-done((bf16[8,128,1024]{2,1,0:T(8,128)(2,1)S(1)}, bf16[8,128,1024]{2,1,0:T(8,128)(2,1)}, u32[]{:S(2)}) %copy-start.2) | copy-done | bytes 2097176
  4.1 0.0 copy-start.3
  4.1 0.9 %copy-done.3 = bf16[8,8192]{1,0:T(8,128)(2,1)S(1)} copy-done((bf16[8,8192]{1,0:T(8,128)(2,1)S(1)}, bf16[8,8192]{1,0:T(8,128)(2,1)}, u32[]{:S(2)}) %copy-start.3) | copy-done | bytes 131096
  5.0 0.0 copy-start.4
  5.0 0.8 %copy-done.4 = bf16[8,2048]{1,0:T(8,128)(2,1)S(1)} copy-done((bf16[8,2048]{1,0:T(8,128)(2,1)S(1)}, bf16[8,2048]{1,0:T(8,128)(2,1)}, u32[]{:S(2)}) %copy-start.4) | copy-done | bytes 32792
  5.8 0.0 copy-start.5
  5.8 0.7 %copy-done.5 = bf16[8,1024]{1,0:T(8,128)(2,1)S(1)} copy-done((bf16[8,1024]{1,0:T(8,128)(2,1)S(1)}, bf16[8,1024]{1,0:T(8,128)(2,1)}, u32[]{:S(2)}) %copy-start.5) | copy-done | bytes 16408
  6.5 0.0 copy-start.7
  6.5 0.7 %copy-done.7 = s32[8]{0:T(128)S(1)} copy-done((s32[8]{0:T(128)S(1)}, s32[8]{0:T(128)}, u32[]{:S(2)}) %copy-start.7) | copy-done | bytes 56
  7.2 0.0 copy-start.8
  7.2 0.7 %copy-done.8 = s32[8,1]{0,1:T(1,128)S(1)} copy-done((s32[8,1]{0,1:T(1,128)S(1)}, s32[8,1]{0,1:T(1,128)}, u32[]{:S(2)}) %copy-start.8) | copy-done | bytes 56
  7.8 0.0 copy-start.9
  7.8 0.7 %copy-done.9 = s32[8]{0:T(128)S(1)} copy-done((s32[8]{0:T(128)S(1)}, s32[8]{0:T(128)}, u32[]{:S(2)}) %copy-start.9) | copy-done | bytes 56
  8.5 11.5 %attend.1 = (s32[4,8,128]{2,1,0:T(8,128)S(1)}, bf16[4,16,1024]{2,1,0:T(8,128)(2,1)S(1)}, bf16[4,128,128]{2,1,0:T(8,128)(2,1)S(1)}, f32[4,8,128]{2,1,0:T(8,128)S(1)}, f32[8,128]{1,0:T(8,128)S(1)}) custom-call(s32[8]{0:T(128)S(1)} %copy-done.7, s32[8]{0:T(128)S(1)} %bitcast.1, s32[8]{0:T(128)S(1)} %copy-done.9, bf16[8,2048]{1,0:T(8,128)(2,1)S(1)} %copy-done.4, ...), custom_call_target="tpu_custom_call" | custom-call | tf_op jit(solution)/shard_map/attend/pallas_call | solution.py:585
  19.9 0.0 copy-done
  19.9 0.0 copy-done.6
  20.0 3.1 %adapters.1 = (f32[4,1,128]{2,1,0:T(1,128)S(1)}, bf16[4,32,256]{2,1,0:T(8,128)(2,1)S(1)}, f32[4,8,256]{2,1,0:T(8,128)S(1)}, f32[8,128]{1,0:T(8,128)S(1)}) custom-call(s32[4,8,128]{2,1,0:T(8,128)S(1)} %get-tuple-element.11.ids_in, bf16[4,16,1024]{2,1,0:T(8,128)(2,1)S(1)} %get-tuple-element.12.hidden_all, s32[2048]{0:T(1024)S(1)} %copy-done.6, ...), custom_call_target="tpu_custom_call" | custom-call | tf_op jit(solution)/shard_map/adapters/pallas_call | solution.py:631
  23.1 12.2 %finish.1 = (bf16[8,1024]{1,0:T(8,128)(2,1)S(1)}, bf16[8,2048]{1,0:T(8,128)(2,1)S(1)}) custom-call(f32[4,1,128]{2,1,0:T(1,128)S(1)} %get-tuple-element.13.low, bf16[4,32,256]{2,1,0:T(8,128)(2,1)S(1)} %get-tuple-element.14.up, f32[4,8,256]{2,1,0:T(8,128)S(1)} %get-tuple-element.15.base, f32[8,128]{1,0:T(8,128)S(1)} %get-tuple-element.16.mask, ...), custom_call_target="tpu_custom_call" | custom-call | tf_op jit(solution)/shard_map/finish/pallas_call | solution.py:663
  35.3 0.6 %copy.16 = bf16[8,1024]{1,0:T(8,128)(2,1)} copy(bf16[8,1024]{1,0:T(8,128)(2,1)S(1)} %get-tuple-element.22) | data formatting | bytes 32768
  35.9 0.6 %copy.17 = bf16[8,2048]{1,0:T(8,128)(2,1)} copy(bf16[8,2048]{1,0:T(8,128)(2,1)S(1)} %get-tuple-element.23) | data formatting | bytes 65536
  (1 shorter events, 0.0 us)
Async XLA Ops:
  0.6 19.3 %copy-start = (bf16[2048,1024]{1,0:T(8,128)(2,1)S(1)}, bf16[2048,1024]{1,0:T(8,128)(2,1)}, u32[]{:S(2)}) copy-start(bf16[2048,1024]{1,0:T(8,128)(2,1)} %weight.1) | copy-start | bytes 12582916
  0.6 1.7 %copy-start.1 = (bf16[8,128,1024]{2,1,0:T(8,128)(2,1)S(1)}, bf16[8,128,1024]{2,1,0:T(8,128)(2,1)}, u32[]{:S(2)}) copy-start(bf16[8,128,1024]{2,1,0:T(8,128)(2,1)} %keys.1) | copy-start | bytes 6291460
  2.4 1.7 %copy-start.2 = (bf16[8,128,1024]{2,1,0:T(8,128)(2,1)S(1)}, bf16[8,128,1024]{2,1,0:T(8,128)(2,1)}, u32[]{:S(2)}) copy-start(bf16[8,128,1024]{2,1,0:T(8,128)(2,1)} %values.1) | copy-start | bytes 6291460
  4.1 0.9 %copy-start.3 = (bf16[8,8192]{1,0:T(8,128)(2,1)S(1)}, bf16[8,8192]{1,0:T(8,128)(2,1)}, u32[]{:S(2)}) copy-start(bf16[8,8192]{1,0:T(8,128)(2,1)} %query.1) | copy-start | bytes 393220
  5.0 0.8 %copy-start.4 = (bf16[8,2048]{1,0:T(8,128)(2,1)S(1)}, bf16[8,2048]{1,0:T(8,128)(2,1)}, u32[]{:S(2)}) copy-start(bf16[8,2048]{1,0:T(8,128)(2,1)} %hidden.1) | copy-start | bytes 98308
  5.8 0.7 %copy-start.5 = (bf16[8,1024]{1,0:T(8,128)(2,1)S(1)}, bf16[8,1024]{1,0:T(8,128)(2,1)}, u32[]{:S(2)}) copy-start(bf16[8,1024]{1,0:T(8,128)(2,1)} %new_keys.1) | copy-start | bytes 49156
  6.5 0.7 %copy-start.7 = (s32[8]{0:T(128)S(1)}, s32[8]{0:T(128)}, u32[]{:S(2)}) copy-start(s32[8]{0:T(128)} %wanted.1) | copy-start | bytes 100
  7.2 0.7 %copy-start.8 = (s32[8,1]{0,1:T(1,128)S(1)}, s32[8,1]{0,1:T(1,128)}, u32[]{:S(2)}) copy-start(s32[8,1]{0,1:T(1,128)} %param.18) | copy-start | bytes 100
  7.8 0.7 %copy-start.9 = (s32[8]{0:T(128)S(1)}, s32[8]{0:T(128)}, u32[]{:S(2)}) copy-start(s32[8]{0:T(128)} %lengths.1) | copy-start | bytes 100
  8.5 11.5 %copy-start.6 = (s32[2048]{0:T(1024)S(1)}, s32[2048]{0:T(1024)}, u32[]{:S(2)}) copy-start(s32[2048]{0:T(1024)} %table_in.1) | copy-start | bytes 24580

commit v3 on v2

--- a/solution.py
+++ b/solution.py
@@ -15,9 +15,8 @@
 BF16 = jnp.bfloat16
 MESH = pl.DeviceIdType.MESH
 VMEM = pl.BlockSpec(memory_space=pltpu.VMEM)
-HBM = pl.BlockSpec(memory_space=pltpu.HBM)
 ANY = pl.BlockSpec(memory_space=pl.ANY)
-ROOM = 48 * 1024 * 1024
+ROOM = 60 * 1024 * 1024
 
 
 def dot_nt(a, b):
@@ -41,11 +40,13 @@
     new_keys,
     keys,
     values,
+    weight,
     ids_out,
     hidden_out,
     acc_out,
     stats_out,
     fresh_out,
+    base_out,
     wanted_s,
     picks_s,
     lengths_s,
@@ -54,11 +55,18 @@
     new_keys_v,
     key_buf,
     value_buf,
+    weight_buf,
+    ids_v,
+    packed_v,
     acc_send,
     stats_send,
+    fresh_v,
+    base_v,
     small_sems,
     key_sems,
     value_sems,
+    weight_sems,
+    own_sems,
     req_send,
     req_recv,
     tp_send,
@@ -121,27 +129,50 @@
         for copy in cache_copies(d if inner else d - 1):
             copy.start()
 
+    pieces = weight_sems.shape[0]
+    deep = depth // pieces
+
+    def weight_copy(c):
+        part = pl.ds(c * deep, deep)
+        return pltpu.make_async_copy(weight.at[part, :], weight_buf.at[part, :], weight_sems.at[c])
+
+    for c in range(pieces):
+        weight_copy(c).start()
+    own = [
+        pltpu.make_async_copy(source, landing, own_sems.at[n])
+        for n, (source, landing) in enumerate(
+            (
+                (ids_v, ids_out.at[me]),
+                (packed_v, hidden_out.at[me]),
+                (acc_send.at[tp], acc_out.at[tp]),
+                (stats_send.at[tp], stats_out.at[tp]),
+                (fresh_v, fresh_out),
+                (base_v, base_out),
+            )
+        )
+    ]
+
     for copy in small[:3]:
         copy.wait()
     wide_rows = hidden_v[...].astype(F32)
-    hidden_out[me] = jnp.concatenate([wide_rows[:, :half], wide_rows[:, half:]], axis=0).astype(
-        BF16
-    )
+    packed_v[...] = jnp.concatenate([wide_rows[:, :half], wide_rows[:, half:]], axis=0).astype(BF16)
     entries = wanted_s.shape[0]
     lane = lax.broadcasted_iota(jnp.int32, (entries, 128), 1)
     sub = lax.broadcasted_iota(jnp.int32, (entries, 128), 0)
     ids = jnp.zeros((entries, 128), jnp.int32)
     for e in range(entries):
         ids = jnp.where(sub == e, jnp.where(lane == 0, picks_s[e], wanted_s[e]), ids)
-    ids_out[me] = ids
+    ids_v[...] = ids
+    for copy in own[:2]:
+        copy.start()
     pl.semaphore_wait(barrier, groups + parts - 2)
 
     def request(n, d):
         peer = lax.rem(me + d, groups)
-        ref = (ids_out, hidden_out)[n]
+        source, landing = ((ids_v, ids_out), (packed_v, hidden_out))[n]
         return pltpu.make_async_remote_copy(
-            src_ref=ref.at[me],
-            dst_ref=ref.at[me],
+            src_ref=source,
+            dst_ref=landing.at[me],
             send_sem=req_send.at[n, d],
             recv_sem=req_recv.at[n, d],
             device_id={"req": peer},
@@ -252,8 +283,8 @@
 
     lax.fori_loop(1, parts, step, 0)
     attend(parts)
-    acc_out[tp] = acc_send[tp]
-    stats_out[tp] = stats_send[tp]
+    for copy in own[2:4]:
+        copy.start()
 
     fresh = jnp.zeros((rows, 128), F32)
     for j in range(here):
@@ -262,53 +293,63 @@
             F32
         )
         fresh = jnp.where(lane == j, jnp.sum(both, axis=1, keepdims=True) * scale, fresh)
-    fresh_out[...] = fresh
+    fresh_v[...] = fresh
+    own[4].start()
+    base = jnp.zeros((rows, kv_width), F32)
+    for c in range(pieces):
+        weight_copy(c).wait()
+        part = slice(c * deep, (c + 1) * deep)
+        base = base + jnp.dot(hidden_v[:, part], weight_buf[part, :], preferred_element_type=F32)
+    share_cols = base_v.shape[2]
+    for p in range(parts):
+        base_v[p] = base[:, p * share_cols : (p + 1) * share_cols]
+    own[5].start()
     lax.fori_loop(1, groups, request_wait, 0)
     lax.fori_loop(1, parts, share_wait, 0)
+    for copy in own:
+        copy.wait()
 
 
 def adapter_kernel(
     groups,
     parts,
     ids_in,
-    hidden_all,
+    hidden_in,
     table_in,
-    weight,
     down,
     up,
     low_out,
     up_out,
-    base_out,
     mask_out,
     ids,
     table,
-    weight_buf,
+    hidden_all,
     down_buf,
+    low_v,
+    up_v,
+    mask_v,
     slots,
     small_sems,
-    weight_sems,
     down_sems,
     up_sems,
 ):
     me = lax.axis_index("req")
-    depth, kv_width = weight.shape
+    depth = down.shape[2]
     rows = hidden_all.shape[1] // 2
     store = down.shape[0]
     entries = ids.shape[1]
-    columns = up.shape[2]
     half = depth // 2
-    pieces = weight_sems.shape[0]
-    tall = depth // pieces
     width = mask_out.shape[1]
 
     small = [
         pltpu.make_async_copy(ids_in, ids, small_sems.at[0]),
         pltpu.make_async_copy(table_in, table, small_sems.at[1]),
+        pltpu.make_async_copy(hidden_in, hidden_all, small_sems.at[2]),
     ]
-
-    def weight_copy(c):
-        part = pl.ds(c * tall, tall)
-        return pltpu.make_async_copy(weight.at[part, :], weight_buf.at[part, :], weight_sems.at[c])
+    results = [
+        pltpu.make_async_copy(source, landing, small_sems.at[3 + n])
+        for n, (source, landing) in enumerate(((low_v, low_out), (up_v, up_out), (mask_v, mask_out)))
+    ]
 
     def down_copy(place, slot):
         part = pl.ds(slot * ADAPTER_RANK, ADAPTER_RANK)
@@ -317,15 +358,13 @@
     def up_copy(place, slot):
         part = pl.ds(lax.rem(slot, CAP) * ADAPTER_RANK, ADAPTER_RANK)
         return pltpu.make_async_copy(
-            up.at[place], up_out.at[slot // CAP, part, :], up_sems.at[slot]
+            up.at[place], up_v.at[slot // CAP, part, :], up_sems.at[slot]
         )
 
     for copy in small:
         copy.start()
-    for c in range(pieces):
-        weight_copy(c).start()
-    up_out[...] = jnp.zeros_like(up_out)
-    for copy in small:
+    up_v[...] = jnp.zeros_like(up_v)
+    for copy in small[:2]:
         copy.wait()
 
     counts = []
@@ -356,20 +395,8 @@
     place = jnp.full((rows, width), -1, jnp.int32)
     for r in range(rows):
         place = jnp.where(slot_row == r, slots[groups * entries + ids[me, r, 0]], place)
-    mask_out[...] = jnp.where(place == slot_lane, 1.0, 0.0)
-
-    own = hidden_all[me]
-    base = [jnp.zeros((2 * rows, kv_width), F32) for _ in range(2)]
-    for c in range(pieces):
-        weight_copy(c).wait()
-        side, at = divmod(c * tall, half)
-        base[side] = base[side] + jnp.dot(
-            own[:, at : at + tall], weight_buf[c * tall : (c + 1) * tall, :],
-            preferred_element_type=F32,
-        )
-    both = base[0][:rows] + base[1][rows:]
-    for p in range(parts):
-        base_out[p] = both[:, p * columns : (p + 1) * columns]
+    mask_v[...] = jnp.where(place == slot_lane, 1.0, 0.0)
+    results[2].start()
 
     for g in range(groups):
         for c in range(CAP):
@@ -379,6 +406,8 @@
                 down_copy(0, g * CAP + c).wait()
                 up_copy(0, g * CAP + c).wait()
 
+    results[1].start()
+    small[2].wait()
     h_all = hidden_all[...].reshape(groups * 2 * rows, half)
     left = dot_nt(h_all, down_buf[:, :half])
     right = dot_nt(h_all, down_buf[:, half:])
@@ -394,9 +423,10 @@
         folded = low[:, :128]
         for c in range(1, width // 128):
             folded = folded + low[:, c * 128 : (c + 1) * 128]
-        low_out[g] = jnp.sum(
-            jnp.where(lane == sub, repeated(folded), 0.0), axis=0, keepdims=True
-        )
+        low_v[g] = jnp.sum(jnp.where(lane == sub, repeated(folded), 0.0), axis=0, keepdims=True)
+    results[0].start()
+    for copy in results:
+        copy.wait()
 
 
 def finish_kernel(
@@ -416,6 +446,11 @@
     base_recv,
     value_recv,
     value_heads,
+    mask_v,
+    acc_v,
+    stats_v,
+    fresh_v,
+    own_sems,
     low_send_sems,
     low_recv_sems,
     up_send_sems,
@@ -444,9 +479,22 @@
         return 0
 
     lax.fori_loop(1, total, greet, 0)
-    low_recv[mine] = low[me]
-    up_recv[me] = up[me]
-    base_recv[tp] = base[tp]
+    own = [
+        pltpu.make_async_copy(source, landing, own_sems.at[n])
+        for n, (source, landing) in enumerate(
+            (
+                (stats, stats_v),
+                (fresh, fresh_v),
+                (acc, acc_v),
+                (base.at[tp], base_recv.at[tp]),
+                (low.at[me], low_recv.at[mine]),
+                (up.at[me], up_recv.at[me]),
+                (mask, mask_v),
+            )
+        )
+    ]
+    for copy in own:
+        copy.start()
 
     def low_copy(o):
         peer = member(o)
@@ -495,16 +543,18 @@
     each(groups, lambda d: up_copy(d).start())
     each(total, lambda o: low_copy(o).start())
 
-    fresh_score = fresh[...]
+    for copy in own[:3]:
+        copy.wait()
+    fresh_score = fresh_v[...]
     peak = fresh_score
     for p in range(parts):
-        peak = jnp.maximum(peak, stats[p])
+        peak = jnp.maximum(peak, stats_v[p])
     fresh_weight = jnp.exp(fresh_score - peak)
     den = fresh_weight
     weights = []
     for p in range(parts):
-        weight = jnp.exp(stats[p] - peak)
-        den = den + weight * pltpu.roll(stats[p], 64, axis=1)
+        weight = jnp.exp(stats_v[p] - peak)
+        den = den + weight * pltpu.roll(stats_v[p], 64, axis=1)
         weights.append(weight)
     inverse = 1.0 / den
     fresh_weight = fresh_weight * inverse
@@ -512,13 +562,15 @@
     old = []
     for j in range(here):
         if (j * rows) % 16 == 0:
-            pair = [acc[p, j * rows : (j + 2) * rows, :].astype(F32) for p in range(parts)]
+            pair = [acc_v[p, j * rows : (j + 2) * rows, :].astype(F32) for p in range(parts)]
         at = (j * rows) % 16
         part = jnp.zeros((rows, HD), F32)
         for p in range(parts):
             part = part + weights[p][:, j : j + 1] * pair[p][at : at + rows]
         old.append(part)
 
+    for copy in own[3:]:
+        copy.wait()
     each(parts, lambda d: tp_copy(0, d).wait_recv())
     base_sum = base_recv[0]
     for p in range(1, parts):
@@ -529,7 +581,7 @@
     lane = lax.broadcasted_iota(jnp.int32, (rows, 128), 1) // ADAPTER_RANK
     sub = lax.broadcasted_iota(jnp.int32, (rows, 128), 0)
     by_row = repeated(jnp.where(lane == sub, jnp.broadcast_to(rank_sum, (rows, 128)), 0.0))
-    low_rank = jnp.concatenate([by_row] * (width // 128), axis=1) * mask[...]
+    low_rank = jnp.concatenate([by_row] * (width // 128), axis=1) * mask_v[...]
     coarse = low_rank.astype(BF16)
     fine = (low_rank - coarse.astype(F32)).astype(BF16)
     matrices = up_recv[...].reshape(width, columns)
@@ -582,7 +634,8 @@
     dma = pltpu.SemaphoreType.DMA
     shape = jax.ShapeDtypeStruct
 
-    ids_all, hidden_all, acc, stats, fresh = pl.pallas_call(
+    pieces = 4 if depth % 1024 == 0 else 2
+    ids_all, hidden_all, acc, stats, fresh, base = pl.pallas_call(
         functools.partial(attend_kernel, groups, parts),
         out_shape=(
             shape((groups, entries, 128), jnp.int32),
@@ -590,9 +643,10 @@
             shape((parts, here * rows, HD), BF16),
             shape((parts, rows, 128), F32),
             shape((rows, 128), F32),
+            shape((parts, rows, columns), F32),
         ),
-        in_specs=[HBM] * 8,
-        out_specs=(VMEM,) * 5,
+        in_specs=[ANY] * 9,
+        out_specs=(ANY,) * 6,
         scratch_shapes=[
             pltpu.SMEM((entries,), jnp.int32),
             pltpu.SMEM((rows,), jnp.int32),
@@ -602,11 +656,18 @@
             pltpu.VMEM(new_token_keys.shape, BF16),
             pltpu.VMEM(cached_key_rows.shape, BF16),
             pltpu.VMEM(cached_value_rows.shape, BF16),
+            pltpu.VMEM(value_projection_weight.shape, BF16),
+            pltpu.VMEM((entries, 128), jnp.int32),
+            pltpu.VMEM((2 * rows, depth // 2), BF16),
             pltpu.VMEM((parts, here * rows, HD), BF16),
             pltpu.VMEM((parts, rows, 128), F32),
+            pltpu.VMEM((rows, 128), F32),
+            pltpu.VMEM((parts, rows, columns), F32),
             dma((6,)),
             dma((chunks,)),
             dma((chunks,)),
+            dma((pieces,)),
+            dma((6,)),
             dma((2, groups)),
             dma((2, groups)),
             dma((2, parts)),
@@ -625,27 +686,28 @@
         new_token_keys,
         cached_key_rows,
         cached_value_rows,
+        value_projection_weight,
     )
 
-    pieces = 4 if depth % 1024 == 0 else 2
-    low, up, base, mask = pl.pallas_call(
+    low, up, mask = pl.pallas_call(
         functools.partial(adapter_kernel, groups, parts),
         out_shape=(
             shape((groups, 1, 128), F32),
             shape((groups, CAP * ADAPTER_RANK, columns), BF16),
-            shape((parts, rows, columns), F32),
             shape((rows, slot_rows), F32),
         ),
-        in_specs=[ANY, VMEM] + [HBM] * 4,
-        out_specs=(VMEM,) * 4,
+        in_specs=[ANY] * 5,
+        out_specs=(ANY,) * 3,
         scratch_shapes=[
             pltpu.SMEM((groups, entries, 128), jnp.int32),
             pltpu.SMEM(adapter_store_row.shape, jnp.int32),
-            pltpu.VMEM(value_projection_weight.shape, BF16),
+            pltpu.VMEM((groups, 2 * rows, depth // 2), BF16),
             pltpu.VMEM((slot_rows, depth), BF16),
+            pltpu.VMEM((groups, 1, 128), F32),
+            pltpu.VMEM((groups, CAP * ADAPTER_RANK, columns), BF16),
+            pltpu.VMEM((rows, slot_rows), F32),
             pltpu.SMEM(((groups + 1) * entries,), jnp.int32),
-            dma((2,)),
-            dma((pieces,)),
+            dma((6,)),
             dma((groups * CAP,)),
             dma((groups * CAP,)),
         ],
@@ -655,7 +717,6 @@
         ids_all,
         hidden_all,
         adapter_store_row,
-        value_projection_weight,
         adapter_down_weight,
         adapter_up_weight,
     )
@@ -663,7 +724,7 @@
     return pl.pallas_call(
         functools.partial(finish_kernel, groups, parts),
         out_shape=(shape((rows, kv_width), BF16), shape((rows, here * HD), BF16)),
-        in_specs=[VMEM] * 7,
+        in_specs=[ANY] * 7,
         out_specs=(VMEM, VMEM),
         scratch_shapes=[
             pltpu.VMEM((total, 1, 128), F32),
@@ -671,6 +732,11 @@
             pltpu.VMEM((parts, rows, columns), F32),
             pltpu.VMEM((parts, rows, columns), F32),
             pltpu.VMEM((kv_heads, rows, HD), F32),
+            pltpu.VMEM(mask.shape, F32),
+            pltpu.VMEM(acc.shape, BF16),
+            pltpu.VMEM(stats.shape, F32),
+            pltpu.VMEM(fresh.shape, F32),
+            dma((7,)),
             dma((total,)),
             dma((total,)),
             dma((groups,)),

time: 36.8 us -> 32.2 us (0.88)
  local copies, waits for them, and re-layouts: 9.04 us -> 2.7 us
  Pallas kernels: 26.7 us -> 28.5 us
    unnamed x22 -> x2, local copies, waits for them, and re-layouts: 9.04 us -> 2.7 us
    pallas_call x1, Pallas kernels: 11.5 us -> 13.2 us  [per_device(): pl.pallas_call(functools.partial(attend_kernel, groups, parts), out_shape...]
    pallas_call x1, Pallas kernels: 3.14 us -> 3.67 us  [per_device(): pl.pallas_call(functools.partial(adapter_kernel, groups, parts), out_shap...]
    pallas_call x1, Pallas kernels: 12.2 us -> 11.7 us  [per_device(): pl.pallas_call(functools.partial(finish_kernel, groups, parts), out_shape...]
where the time goes in v3:
time: 32.2 us; the launch traced here: 31.9 us
  Pallas kernels  28.5 us (89%)
  local copies, waits for them, and re-layouts  2.7 us (8%)
  between operations  0.66 us (2%)
    pallas_call x1, Pallas kernels, per_device(): pl.pallas_call(functools.partial(attend_kernel, groups, parts), out_shape...  13.2 us
    pallas_call x1, Pallas kernels, per_device(): pl.pallas_call(functools.partial(finish_kernel, groups, parts), out_shape...  11.7 us
    pallas_call x1, Pallas kernels, per_device(): pl.pallas_call(functools.partial(adapter_kernel, groups, parts), out_shap...  3.67 us
    unnamed x2, local copies, waits for them, and re-layouts  2.7 us

profile of v3, /device:TPU:0, one launch (start us, length us, event | category | flops | bytes accessed | tf_op | source)
XLA Modules:
  0.0 31.9 jit_solution(10396569558063943543)
XLA Ops:
  0.6 13.2 %attend.1 = (s32[4,8,128]{2,1,0:T(8,128)}, bf16[4,16,1024]{2,1,0:T(8,128)(2,1)}, bf16[4,128,128]{2,1,0:T(8,128)(2,1)}, f32[4,8,128]{2,1,0:T(8,128)}, f32[8,128]{1,0:T(8,128)}, /*index=5*/f32[4,8,256]{2,1,0:T(8,128)}) custom-call(s32[8]{0:T(128)} %wanted.1, s32[8]{0:T(128)} %bitcast.1, s32[8]{0:T(128)} %lengths.1, bf16[8,2048]{1,0:T(8,128)(2,1)} %hidden.1, ...), custom_call_target="tpu_custom_call" | custom-call | tf_op jit(solution)/shard_map/attend/pallas_call | solution.py:638
  13.8 3.7 %adapters.1 = (f32[4,1,128]{2,1,0:T(1,128)}, bf16[4,32,256]{2,1,0:T(8,128)(2,1)}, f32[8,128]{1,0:T(8,128)}) custom-call(s32[4,8,128]{2,1,0:T(8,128)} %get-tuple-element.11.ids_in, bf16[4,16,1024]{2,1,0:T(8,128)(2,1)} %get-tuple-element.12.hidden_in, s32[2048]{0:T(1024)} %table_in.1, bf16[512,16,2048]{2,1,0:T(8,128)(2,1)} %down.1, bf16[512,16,256]{2,1,0:T(8,128)(2,1)} %up.1), custom_call_target="tpu_custom_call" | custom-call | tf_op jit(solution)/shard_map/adapters/pallas_call | solution.py:692
  17.5 11.7 %finish.1 = (bf16[8,1024]{1,0:T(8,128)(2,1)}, bf16[8,2048]{1,0:T(8,128)(2,1)}) custom-call(f32[4,1,128]{2,1,0:T(1,128)} %get-tuple-element.13.low, bf16[4,32,256]{2,1,0:T(8,128)(2,1)} %get-tuple-element.14.up, f32[4,8,256]{2,1,0:T(8,128)} %get-tuple-element.15.base, f32[8,128]{1,0:T(8,128)} %get-tuple-element.16.mask, ...), custom_call_target="tpu_custom_call" | custom-call | tf_op jit(solution)/shard_map/finish/pallas_call | solution.py:724
  29.2 1.3 %copy.16 = bf16[8,1024]{1,0:T(8,128)(2,1)} copy(bf16[8,1024]{1,0:T(8,128)(2,1)} %get-tuple-element.22) | data formatting | bytes 32768
  30.5 1.4 %copy.17 = bf16[8,2048]{1,0:T(8,128)(2,1)} copy(bf16[8,2048]{1,0:T(8,128)(2,1)} %get-tuple-element.23) | data formatting | bytes 65536
